TPU v7x, 256 devices: a whole 4x4x8 slice. The times are simulated.
256 devices in a mesh: ctx: 64 (over z, y, x_hi), tp: 4 (over x_lo, core).
Axes of the slice: x: 4 (x_hi: 2, x_lo: 2; x = x_hi * 2 + x_lo), y: 4, z: 8, core: 2. Of those that a mesh axis runs over, the one named last changes fastest.
Arguments:
- features: bfloat16 [3, 16384, 8192], P(None, 'ctx', 'tp'), may hold values from -6 to 6
- short_weight: float32 [3, 3, 8192], P(None, None, 'tp'), may hold values from -2.5 to 2.5
- filters: float32 [512, 16384], P(('tp', 'ctx')), may hold values from -2 to 2, as said below
- out_weight: bfloat16 [8192, 4096], P(('tp', 'ctx')), may hold values from -0.0625 to 0.0625
Outputs:
- projected: bfloat16 [16384, 4096], P('ctx', 'tp')
Inputs may be any that keep to these rules, and one draw needn't show every extreme that they name: `filters`: real values.
All inputs are finite; a program needn't handle non-finite values.
Results may differ from a plain program's by a relative error of at most 0.015.
Values may be sent and summed in bfloat16 or wider, within the bound.
No kernel may reach another device: no remote copies, remote signals or barrier semaphores. Data moves between devices by JAX's collectives and lax.ppermute only.
A program may use at most 128 MiB of HBM per device.

v0:
```python
import math

import jax
import jax.numpy as jnp
from jax import lax
from jax.sharding import PartitionSpec as P

PRECISE = lax.Precision.HIGH


def shifted(block, axis, distance):
    devices = range(lax.axis_size(axis))
    route = [(i - distance, i) for i in devices if i - distance in devices]
    return lax.ppermute(block, axis, route)


def angles(num_rows, num_cols, period):
    turn_count = (
        lax.broadcasted_iota(jnp.int32, (num_rows, num_cols), 0)
        * lax.broadcasted_iota(jnp.int32, (num_rows, num_cols), 1)
        % period
    )
    return turn_count.astype(jnp.float32) * (2.0 * math.pi / period)


def contract(pattern, left_side, right_side):
    return jnp.einsum(pattern, left_side, right_side, precision=PRECISE)


def forward(signal, first_len, second_len):
    half_len = first_len // 2
    outer_angle = angles(half_len, first_len, first_len)
    real_part = contract("cnb,nk->ckb", signal, jnp.cos(outer_angle))
    imag_part = -contract("cnb,nk->ckb", signal, jnp.sin(outer_angle))
    twist_angle = angles(first_len, second_len, first_len * second_len)
    twist_cos = jnp.cos(twist_angle)
    twist_sin = jnp.sin(twist_angle)
    real_part, imag_part = (
        real_part * twist_cos + imag_part * twist_sin,
        imag_part * twist_cos - real_part * twist_sin,
    )
    inner_angle = angles(second_len, second_len, second_len)
    inner_cos = jnp.cos(inner_angle)
    inner_sin = jnp.sin(inner_angle)
    spec_real = contract("ckb,bj->ckj", real_part, inner_cos) + contract(
        "ckb,bj->ckj", imag_part, inner_sin
    )
    spec_imag = contract("ckb,bj->ckj", imag_part, inner_cos) - contract(
        "ckb,bj->ckj", real_part, inner_sin
    )
    return (spec_real, spec_imag)


def inverse(spec_real, spec_imag, first_len, second_len):
    half_len = first_len // 2
    inner_angle = angles(second_len, second_len, second_len)
    inner_cos = jnp.cos(inner_angle)
    inner_sin = jnp.sin(inner_angle)
    real_part = contract("ckj,jm->ckm", spec_real, inner_cos) - contract(
        "ckj,jm->ckm", spec_imag, inner_sin
    )
    imag_part = contract("ckj,jm->ckm", spec_real, inner_sin) + contract(
        "ckj,jm->ckm", spec_imag, inner_cos
    )
    twist_angle = angles(first_len, second_len, first_len * second_len)
    twist_cos = jnp.cos(twist_angle)
    twist_sin = jnp.sin(twist_angle)
    real_part, imag_part = (
        real_part * twist_cos - imag_part * twist_sin,
        real_part * twist_sin + imag_part * twist_cos,
    )
    outer_angle = angles(first_len, half_len, first_len)
    values = contract("ckm,kn->cnm", real_part, jnp.cos(outer_angle)) - contract(
        "ckm,kn->cnm", imag_part, jnp.sin(outer_angle)
    )
    return values / float(first_len * second_len)


def long_conv(signal, filters):
    length, channels = signal.shape
    second_len = math.gcd(length, 128)
    first_len = 2 * length // second_len
    half_len = first_len // 2
    groups = filters.shape[0]
    per_group = channels // groups
    series = signal.astype(jnp.float32).T.reshape(channels, half_len, second_len)
    data_real, data_imag = forward(series, first_len, second_len)
    filt_real, filt_imag = forward(
        filters.reshape(groups, half_len, second_len), first_len, second_len
    )
    data_real = data_real.reshape(groups, per_group, first_len, second_len)
    data_imag = data_imag.reshape(groups, per_group, first_len, second_len)
    filt_real = filt_real[:, None]
    filt_imag = filt_imag[:, None]
    prod_real = (data_real * filt_real - data_imag * filt_imag).reshape(
        channels, first_len, second_len
    )
    prod_imag = (data_real * filt_imag + data_imag * filt_real).reshape(
        channels, first_len, second_len
    )
    return inverse(prod_real, prod_imag, first_len, second_len).reshape(channels, length).T


def short_conv(extended, short_weight, token_count):
    mixture = jnp.zeros((extended.shape[0], token_count, extended.shape[2]), jnp.float32)
    for offset in range(short_weight.shape[1]):
        mixture = (
            mixture
            + extended[:, offset : offset + token_count, :].astype(jnp.float32)
            * short_weight[:, offset, None, :]
        )
    return mixture.astype(jnp.bfloat16)


def on_device(features, short_weight, filters, out_weight):
    token_count = features.shape[1]
    rim_rows = short_weight.shape[1] - 1
    before = shifted(features[:, token_count - rim_rows :, :], "ctx", 1)
    featurized = short_conv(jnp.concatenate([before, features], axis=1), short_weight, token_count)
    spread = lax.all_to_all(featurized, "ctx", split_axis=2, concat_axis=1, tiled=True)
    product = (spread[1].astype(jnp.float32) * spread[2].astype(jnp.float32)).astype(jnp.bfloat16)
    convolved = long_conv(product, filters).astype(jnp.bfloat16)
    local_gated = (spread[0].astype(jnp.float32) * convolved.astype(jnp.float32)).astype(
        jnp.bfloat16
    )
    gated_out = lax.all_to_all(local_gated, "ctx", split_axis=0, concat_axis=1, tiled=True)
    partial_value = jnp.dot(
        gated_out,
        lax.all_gather(out_weight, "ctx", axis=0, tiled=True),
        preferred_element_type=jnp.float32,
    )
    return lax.psum_scatter(partial_value, "tp", scatter_dimension=1, tiled=True).astype(
        jnp.bfloat16
    )


def solution(mesh):
    in_specs = (
        P(None, "ctx", "tp"),
        P(None, None, "tp"),
        P(("tp", "ctx"), None),
        P(("tp", "ctx"), None),
    )
    out_specs = P("ctx", "tp")
    return jax.shard_map(
        on_device, mesh=mesh, in_specs=in_specs, out_specs=out_specs, check_vma=False
    )
```

profile of v0, /device:TPU:1, one launch (start us, length us, event | category | flops | bytes accessed | tf_op | source)
XLA Modules:
  0.0 361.9 jit_solution(12304427150519293585)
XLA Ops:
  6.5 0.7 all-gather.2.cloned.1.call-update
  7.3 0.9 slice.30
  8.2 5.5 %collective-permute-start = (bf16[3,2,2048]{2,1,0:T(2,128)(2,1)S(1)}, bf16[3,2,2048]{2,1,0:T(2,128)(2,1)S(1)}, u32[]{:S(2)}, u32[]{:S(2)}) collective-permute-start(bf16[3,2,2048]{2,1,0:T(2,128)(2,1)S(1)} %slice.30), channel_id=1, source_target_pairs={{0,4},{4,8},{8,12},{12,16},{16,20},{20,24},{24,28},{28,32},{32,36}... | collective-permute-start | bytes 73736 | tf_op jit(solution)/shard_map/ppermute | solution.py:14
  13.7 1.1 fusion.190
  14.8 7.2 %copy.35 = bf16[3,256,2048]{1,0,2:T(4,128)(2,1)} copy(bf16[3,256,2048]{2,1,0:T(8,128)(2,1)} %param.4) | data formatting | bytes 6291456 | tf_op args[0]
  22.4 1.3 copy.51
  23.7 1.4 copy.52
  25.2 1.4 copy.34
  26.6 16.9 %add_convert_fusion = bf16[3,256,2048]{1,0,2:T(4,128)(2,1)} fusion(bf16[3,256,2048]{1,0,2:T(4,128)(2,1)} %copy.35, bf16[3,2,2048]{1,0,2:T(4,128)(2,1)S(1)} %copy.34, f32[3,2048]{0,1:T(8,128)} %bitcast.155, f32[3,2048]{0,1:T(8,128)} %bitcast.154, f32[3,2048]{0,1:T(8,128)S(1)} %bitcast.153), kind=kLoop, calls=%fused_computation | loop fusion | flops 23592960 | bytes 6389760 | tf_op jit(solution)/shard_map/convert_element_type | solution.py:112
  43.5 12.9 %all-to-all-start = ((bf16[3,256,2048]{1,0,2:T(4,128)(2,1)}), bf16[3,256,2048]{1,0,2:T(4,128)(2,1)}, u32[]{:S(2)}, u32[]{:S(2)}) async-start(bf16[3,256,2048]{1,0,2:T(4,128)(2,1)} %add_convert_fusion), calls=%async_computation | async-start | bytes 8388608 | tf_op jit(solution)/shard_map/all_to_all | solution.py:120
  60.8 1.2 convolution_subtract_fusion.1
  62.0 112.2 %all-to-all-done = bf16[3,256,2048]{1,0,2:T(4,128)(2,1)} async-done(((bf16[3,256,2048]{1,0,2:T(4,128)(2,1)}), bf16[3,256,2048]{1,0,2:T(4,128)(2,1)}, u32[]{:S(2)}, u32[]{:S(2)}) %all-to-all-start) | async-done | bytes 3145760 | tf_op jit(solution)/shard_map/all_to_all | solution.py:120
  174.2 2.6 copy.40
  177.9 1.5 copy.54
  179.4 1.7 fusion.54
  181.0 1.7 fusion.57
  182.7 2.3 fusion.5
  185.0 2.5 fusion.3
  187.5 2.3 fusion.19
  189.8 3.8 %fusion.1 = (f32[32,256,128]{2,1,0:T(8,128)S(1)}, f32[32,256,128]{2,1,0:T(8,128)S(1)}) fusion(f32[32,256,128]{2,1,0:T(8,128)S(1)} %fusion.19, f32[2,256,128]{2,1,0:T(8,128)} %convolution_subtract_fusion.1, f32[2,256,128]{2,1,0:T(8,128)S(1)} %convolution_add_fusion.1, f32[32,256,128]{2,1,0:T(8,128)S(1)} %fusion.3, f32[256,128]{1,0:T(8,128)S(1)} %copy.44, ...), kind=kOutput, calls=%fused_computation.8 | convolution fusion | flops 817070080 | bytes 25952256 | tf_op jit(solution)/shard_map/ckb,bj->ckj/dot_general | solution.py:27
  193.6 2.0 fusion.85
  195.7 2.0 fusion.77
  197.7 2.5 convolution_subtract_fusion
  200.2 2.0 convolution_add_fusion
  202.2 2.0 fusion.11
  204.3 2.1 fusion.33
  206.4 1.2 fusion.26
  207.8 34.9 %all_to_all.34 = bf16[64,256,32]{1,2,0:T(8,128)(2,1)S(1)} all-to-all(bf16[64,256,32]{1,2,0:T(8,128)(2,1)S(1)} %bitcast.152), channel_id=1, replica_groups=mesh['ctx'=64,'tp'=4] {'ctx'}, dimensions={0} | all-to-all | bytes 2097152 | tf_op jit(solution)/shard_map/all_to_all | solution.py:126
  242.7 54.3 %all-gather.2.cloned.1.call-done = bf16[2048,4096]{1,0:T(8,128)(2,1)} async-done(((bf16[32,4096]{1,0:T(8,128)(2,1)}), bf16[2048,4096]{1,0:T(8,128)(2,1)}) %all-gather.2.cloned.1.call-update) | async-done | bytes 16777232 | tf_op jit(solution)/shard_map/all_gather | solution.py:129
  297.1 10.1 %fusion.193 = f32[256,4096]{1,0:T(8,128)} fusion(bf16[256,2048]{0,1:T(8,128)(2,1)S(1)} %bitcast.149, bf16[2048,4096]{1,0:T(8,128)(2,1)} %all-gather.2.cloned.1.call-done), kind=kOutput, calls=%fused_computation.201 | convolution fusion | flops 4294967296 | bytes 22020096 | tf_op jit(solution)/shard_map/dot_general | solution.py:127
  307.2 45.6 %reduce-scatter.2.cloned.1.call-done = f32[256,1024]{1,0:T(8,128)} async-done(((f32[256,4096]{1,0:T(8,128)}), f32[256,1024]{1,0:T(8,128)}) %reduce-scatter.2.cloned.1.call-update) | async-done | bytes 1048592 | tf_op jit(solution)/shard_map/reduce_scatter | solution.py:132
  352.8 2.1 convert_element_type.153
  (23 shorter events, 5.8 us)
Async XLA Ops:
  6.5 290.5 %all-gather.2.cloned.1.call-start = ((), (), s32[]{:S(2)}) async-start(), calls=%async_computation.3 | async-start | bytes 17039360 | tf_op jit(solution)/shard_map/all_gather | solution.py:129
  8.2 17.0 %collective-permute-start = (bf16[3,2,2048]{2,1,0:T(2,128)(2,1)S(1)}, bf16[3,2,2048]{2,1,0:T(2,128)(2,1)S(1)}, u32[]{:S(2)}, u32[]{:S(2)}) collective-permute-start(bf16[3,2,2048]{2,1,0:T(2,128)(2,1)S(1)} %slice.30), channel_id=1, source_target_pairs={{0,4},{4,8},{8,12},{12,16},{16,20},{20,24},{24,28},{28,32},{32,36}... | collective-permute-start | bytes 73736 | tf_op jit(solution)/shard_map/ppermute | solution.py:14
  43.5 14.3 %copy-start.1 = (f32[2,16384]{1,0:T(2,128)S(1)}, f32[2,16384]{1,0:T(2,128)}, u32[]{:S(2)}) copy-start(f32[2,16384]{1,0:T(2,128)} %param.6) | copy-start | bytes 393220
  43.5 130.7 %all-to-all-start = ((bf16[3,256,2048]{1,0,2:T(4,128)(2,1)}), bf16[3,256,2048]{1,0,2:T(4,128)(2,1)}, u32[]{:S(2)}, u32[]{:S(2)}) async-start(bf16[3,256,2048]{1,0,2:T(4,128)(2,1)} %add_convert_fusion), calls=%async_computation | async-start | bytes 8388608 | tf_op jit(solution)/shard_map/all_to_all | solution.py:120
  56.4 296.4 %reduce-scatter.2.cloned.1.call-start = ((), (), s32[]{:S(2)}) async-start(), calls=%async_computation.4 | async-start | bytes 5242880 | tf_op jit(solution)/shard_map/reduce_scatter | solution.py:132
  204.3 2.1 copy-start
Sparse Core Ops, SparseCore 0:
  11.1 285.9 all-gather.1
  307.3 45.3 reduce-scatter.1
where the time goes:
time: 365 us; the launch traced here: 362 us
  waiting for transfers between devices  213 us (58%)
  matrix products  41.3 us (11%)
  blocking collectives  34.9 us (10%)
  other arithmetic  21.8 us (6%)
  starting transfers between devices  18.6 us (5%)
  local copies, waits for them, and re-layouts  18.6 us (5%)
  between operations  13.9 us (4%)
    all_to_all x1, waiting for transfers between devices, on_device(): lax.all_to_all(featurized, 'ctx', split_axis=2, concat_axis=1, tiled=True)  112 us
    all_gather x1, waiting for transfers between devices, on_device(): lax.all_gather(out_weight, 'ctx', axis=0, tiled=True)  54.3 us
    reduce_scatter x1, waiting for transfers between devices, on_device(): lax.psum_scatter(partial_value, 'tp', scatter_dimension=1, tiled=True)  45.6 us
    all_to_all x1, blocking collectives, on_device(): lax.all_to_all(local_gated, 'ctx', split_axis=0, concat_axis=1, tiled=True)  34.9 us
    dot_general x18, matrix products, contract(): return jnp.einsum(pattern, left_side, right_side, precision=PRECISE)  31.1 us
    convert_element_type x1, other arithmetic, short_conv(): return mixture.astype(jnp.bfloat16)  16.9 us
    all_to_all x1, starting transfers between devices, on_device(): lax.all_to_all(featurized, 'ctx', split_axis=2, concat_axis=1, tiled=True)  12.9 us
    dot_general x1, matrix products, on_device(): jnp.dot(gated_out, lax.all_gather(out_weight, 'ctx', axis=0, tiled=True),...  10.1 us
  transfers between devices with their start and end apart: 4, of which 3 were waited for; matrix products, arithmetic and copies ran while one was open for 19% of the time, Pallas kernels for 0%

commit v1 on v0

v1 whole, which is shorter than its diff:
```python
import functools

import jax
import jax.numpy as jnp
from jax import lax
from jax.experimental import pallas as pl
from jax.experimental.pallas import tpu as pltpu
from jax.sharding import Mesh, PartitionSpec as P

CTX = ("z", "y", "xh")
RING = ("xh", "xl")
F32, BF16 = jnp.float32, jnp.bfloat16
TOK = 256
WIDE = 8
VMEM = 56 * 1024 * 1024


def featurize_kernel(first_ref, x_ref, halo_ref, w_ref, prod_ref, gate_ref):
    rows = lax.broadcasted_iota(jnp.int32, x_ref.shape[1:], 0)
    live = first_ref[0] != 0

    def one(i):
        x = x_ref[i].astype(F32)
        halo = jnp.where(live, halo_ref[i].astype(F32), 0.0)
        x1 = jnp.where(rows == 0, halo[1:2], pltpu.roll(x, 1, 0))
        x2 = jnp.where(rows == 0, halo[0:1], pltpu.roll(x1, 1, 0))
        taps = w_ref[i]
        mix = x2 * taps[0:1] + x1 * taps[1:2] + x * taps[2:3]
        return mix.astype(BF16).astype(F32)

    prod_ref[...] = (one(1) * one(2)).T.astype(BF16)
    gate_ref[...] = one(0).T.astype(BF16)


def featurize(first, features, halo, taps, width=256):
    _, tok, chans = features.shape
    out = jax.ShapeDtypeStruct((chans, tok), BF16)
    return pl.pallas_call(
        featurize_kernel,
        grid=(chans // width,),
        in_specs=[
            pl.BlockSpec(memory_space=pltpu.SMEM),
            pl.BlockSpec((3, tok, width), lambda i: (0, 0, i)),
            pl.BlockSpec((3, 2, width), lambda i: (0, 0, i)),
            pl.BlockSpec((3, 3, width), lambda i: (0, 0, i)),
        ],
        out_specs=[pl.BlockSpec((width, tok), lambda i: (i, 0))] * 2,
        out_shape=[out, out],
        name="featurize",
    )(first, features, halo, taps)


def toeplitz_kernel(h_ref, t_ref):
    step = pl.program_id(1)
    span = TOK * WIDE
    base = pl.multiple_of(step * span, span)
    lags = h_ref[0, :, pl.ds(base, span + TOK)]
    strip = 16
    for i in range(TOK // strip):
        wide = jnp.broadcast_to(lags, (strip, span + TOK))
        slid = pltpu.roll(wide, i * strip, 1, stride=1, stride_axis=0)
        slid = slid.astype(BF16)
        for k in range(WIDE):
            t_ref[0, k, i * strip : (i + 1) * strip, :] = slid[:, (k + 1) * TOK : (k + 2) * TOK]


def toeplitz(filters):
    groups, length = filters.shape
    blocks = length // TOK
    padded = jnp.pad(filters, ((0, 0), (TOK, 0)))[:, None, :]
    return pl.pallas_call(
        toeplitz_kernel,
        grid=(groups, blocks // WIDE),
        in_specs=[pl.BlockSpec((1, 1, length + TOK), lambda g, s: (g, 0, 0))],
        out_specs=pl.BlockSpec((1, WIDE, TOK, TOK), lambda g, s: (g, s, 0, 0)),
        out_shape=jax.ShapeDtypeStruct((groups, blocks, TOK, TOK), BF16),
        cost_estimate=pl.CostEstimate(flops=0, bytes_accessed=48 * 2**20, transcendentals=0),
        name="toeplitz",
    )(padded)


def conv_kernel(per_group, x_ref, t_ref, y_ref, wide_ref, acc_ref):
    step = pl.program_id(1)
    blocks = x_ref.shape[0]
    rows = blocks * per_group

    @pl.when(step == 0)
    def _():
        x = x_ref[...].reshape(rows, TOK)
        for j in range(WIDE):
            lead = j * per_group
            if lead:
                wide_ref[0:lead, j * TOK : (j + 1) * TOK] = jnp.zeros((lead, TOK), BF16)
            wide_ref[lead:, j * TOK : (j + 1) * TOK] = x[: rows - lead]

    t = t_ref[0].reshape(WIDE * TOK, TOK)
    for s in range(blocks // WIDE):

        @pl.when(step == s)
        def _():
            lead = s * WIDE * per_group
            part = jnp.dot(wide_ref[0 : rows - lead, :], t, preferred_element_type=F32)
            if s == 0:
                acc_ref[...] = part
            else:
                acc_ref[lead:, :] += part

    @pl.when(step == blocks // WIDE - 1)
    def _():
        y_ref[...] = acc_ref[...].astype(BF16).reshape(y_ref.shape)


def long_conv(x, t):
    blocks, chans, tok = x.shape
    groups = t.shape[0]
    per_group = chans // groups
    return pl.pallas_call(
        functools.partial(conv_kernel, per_group),
        grid=(groups, blocks // WIDE),
        in_specs=[
            pl.BlockSpec((blocks, per_group, tok), lambda g, s: (0, g, 0)),
            pl.BlockSpec((1, WIDE, TOK, TOK), lambda g, s: (g, s, 0, 0)),
        ],
        out_specs=pl.BlockSpec((blocks, per_group, tok), lambda g, s: (0, g, 0)),
        out_shape=jax.ShapeDtypeStruct(x.shape, BF16),
        scratch_shapes=[
            pltpu.VMEM((blocks * per_group, WIDE * TOK), BF16),
            pltpu.VMEM((blocks * per_group, TOK), F32),
        ],
        compiler_params=pltpu.CompilerParams(vmem_limit_bytes=VMEM),
        cost_estimate=pl.CostEstimate(
            flops=chans * blocks * blocks * tok * tok, bytes_accessed=20 * 2**20, transcendentals=0
        ),
        name="long_conv",
    )(x, t)


def gate_kernel(conv_ref, gate_ref, out_ref):
    gated = conv_ref[...].astype(F32) * gate_ref[...].astype(F32)
    chans = conv_ref.shape[0] * conv_ref.shape[2]
    for x in range(2):
        part = gated[:, x].astype(BF16).astype(F32).reshape(chans, TOK)
        out_ref[x] = part.T.astype(BF16)


def gating(conv, gate):
    srcs, halves, chans, tok = conv.shape
    group = 8
    return pl.pallas_call(
        gate_kernel,
        grid=(srcs // group,),
        in_specs=[pl.BlockSpec((group, halves, chans, tok), lambda i: (i, 0, 0, 0))] * 2,
        out_specs=pl.BlockSpec((halves, tok, group * chans), lambda i: (0, 0, i)),
        out_shape=jax.ShapeDtypeStruct((halves, tok, srcs * chans), BF16),
        name="gating",
    )(conv, gate)


def project_kernel(where_ref, a_ref, w_ref, *refs):
    del where_ref
    a = a_ref[0]
    part = jnp.dot(a, w_ref[...], preferred_element_type=F32)
    if len(refs) == 2:
        part = part + refs[0][0].astype(F32)
    refs[-1][0] = part.astype(BF16)


def project(where, a, w, added=None):
    halves, tok, chans = a.shape
    width = w.shape[1] // 4
    block = pl.BlockSpec((1, tok, width), lambda r, s: (r, 0, 0))
    return pl.pallas_call(
        project_kernel,
        grid_spec=pltpu.PrefetchScalarGridSpec(
            num_scalar_prefetch=1,
            grid=(4,),
            in_specs=[
                pl.BlockSpec((1, tok, chans), lambda r, s: (s[0, r], 0, 0)),
                pl.BlockSpec((chans, width), lambda r, s: (0, s[1, r])),
            ]
            + ([block] if added is not None else []),
            out_specs=block,
        ),
        out_shape=jax.ShapeDtypeStruct((4, tok, width), BF16),
        compiler_params=pltpu.CompilerParams(vmem_limit_bytes=VMEM),
        name="project",
    )(where, a, w, *([added] if added is not None else []))


def on_device(features, short_weight, filters, out_weight):
    tok, chans = features.shape[1:]
    rim = features[:, tok - 2 :, :]
    ctx_size = lax.axis_size(CTX)
    halo = lax.ppermute(rim, CTX, [(i, (i + 1) % ctx_size) for i in range(ctx_size)])
    live = jnp.where(lax.axis_index(CTX) == 0, 0, 1).astype(jnp.int32)[None]
    weights = lax.all_gather(out_weight, ("z", "y"), axis=0, tiled=True)
    product, gate = featurize(live, features, halo, short_weight)
    mine = chans // ctx_size
    series = lax.all_to_all(
        product.reshape(ctx_size, mine, tok), CTX, split_axis=0, concat_axis=0, tiled=True
    )
    blocks = toeplitz(filters)
    xh, xl, core = lax.axis_index("xh"), lax.axis_index("xl"), lax.axis_index("core")
    gate = gate.reshape(ctx_size // 2, 2, mine, tok)
    own = lax.dynamic_index_in_dim(gate, xh, 1, keepdims=False)
    other = lax.dynamic_index_in_dim(gate, 1 - xh, 1, keepdims=False)
    other = lax.ppermute(other, "xh", [(0, 1), (1, 0)])
    gates = jnp.where(xh == 0, jnp.stack([own, other], 1), jnp.stack([other, own], 1))

    convolved = long_conv(series, blocks)
    convolved = convolved.reshape(ctx_size // 2, 2, mine, tok)
    back = lax.all_to_all(convolved, ("z", "y"), split_axis=0, concat_axis=0, tiled=True)
    gated = gating(back, gates)

    place = xh * 2 + xl
    there = (place + jnp.arange(4, dtype=jnp.int32)) % 4
    half, lane = there // 2, there % 2
    out_block = jnp.stack([half, lane * 2 + (1 - core)]).astype(jnp.int32)
    own_block = jnp.stack([half, lane * 2 + core]).astype(jnp.int32)
    passed = project(out_block, gated, weights)
    passed = lax.ppermute(passed, "core", [(0, 1), (1, 0)])
    sums = project(own_block, gated, weights, passed)
    total = sums[0].astype(F32)
    for r in range(1, 4):
        got = lax.ppermute(sums[r], RING, [(i, (i + r) % 4) for i in range(4)])
        total = total + got.astype(F32)
    return total.astype(BF16)


def solution(mesh):
    fine = Mesh(mesh.devices.reshape(8, 4, 2, 2, 2), ("z", "y", "xh", "xl", "core"))
    tp = ("xl", "core")
    in_specs = (
        P(None, CTX, tp),
        P(None, None, tp),
        P(tp + CTX, None),
        P(tp + CTX, None),
    )
    return jax.shard_map(
        on_device, mesh=fine, in_specs=in_specs, out_specs=P(CTX, tp), check_vma=False
    )
```

time: 365 us -> 203 us (0.56)
  waiting for transfers between devices: 213 us -> 94.5 us
  Pallas kernels: 0 us -> 58.2 us
  matrix products: 41.3 us -> 0 us
  blocking collectives: 34.9 us -> 0 us
  other arithmetic: 21.8 us -> 3.99 us
  local copies, waits for them, and re-layouts: 18.6 us -> 7.19 us
  starting transfers between devices: 18.6 us -> 24.5 us
    all_to_all x1 -> x2, waiting for transfers between devices: 112 us -> 46.5 us  [the longest x1 25 us: on_device(): lax.all_to_all(convolved, ('z', 'y'), split_axis=0, concat_axis=0, tiled=...]
    pallas_call x0 -> x6, Pallas kernels: none -> 58.2 us  [the longest x1 20.5 us: long_conv(): pl.pallas_call(functools.partial(conv_kernel, per_group), grid=(groups, b...]
    all_gather x1, waiting for transfers between devices: 54.3 us -> 0.28 us  [on_device(): weights = lax.all_gather(out_weight, ('z', 'y'), axis=0, tiled=True)]
    ppermute x1 -> x6, waiting for transfers between devices: 0.01 us -> 47 us  [the longest x3 22.8 us: on_device(): got = lax.ppermute(sums[r], RING, [(i, (i + r) % 4) for i in range(4)])]
    reduce_scatter x1 -> x0, waiting for transfers between devices: 45.6 us -> none  [on_device(): lax.psum_scatter(partial_value, 'tp', scatter_dimension=1, tiled=True)]
    dot_general x19 -> x0, matrix products: 41.3 us -> none  [the longest x18 31.1 us: contract(): return jnp.einsum(pattern, left_side, right_side, precision=PRECISE)]
    all_to_all x1 -> x0, blocking collectives: 34.9 us -> none  [on_device(): lax.all_to_all(local_gated, 'ctx', split_axis=0, concat_axis=1, tiled=True)]
    convert_element_type x3 -> x1, other arithmetic: 20.2 us -> 2.2 us  [on_device(): return total.astype(BF16)]
  transfers between devices with their start and end apart: 4 -> 9, of which waited for: 3 -> 8; matrix products, arithmetic and copies ran while one was open for 19% -> 2% of each run, Pallas kernels for 0% -> 21%
where the time goes in v1:
time: 203 us; the launch traced here: 202 us
  waiting for transfers between devices  94.5 us (47%)
  Pallas kernels  58.2 us (29%)
  starting transfers between devices  24.5 us (12%)
  between operations  13.5 us (7%)
  local copies, waits for them, and re-layouts  7.19 us (4%)
  other arithmetic  3.99 us (2%)
    all_to_all x1, waiting for transfers between devices, on_device(): lax.all_to_all(convolved, ('z', 'y'), split_axis=0, concat_axis=0, tiled=...  25 us
    ppermute x3, waiting for transfers between devices, on_device(): got = lax.ppermute(sums[r], RING, [(i, (i + r) % 4) for i in range(4)])  22.8 us
    all_to_all x1, waiting for transfers between devices, on_device(): lax.all_to_all(product.reshape(ctx_size, mine, tok), CTX, split_axis=0, c...  21.6 us
    pallas_call x1, Pallas kernels, long_conv(): pl.pallas_call(functools.partial(conv_kernel, per_group), grid=(groups, b...  20.5 us
    pallas_call x2, Pallas kernels, project(): pl.pallas_call(project_kernel, grid_spec=pltpu.PrefetchScalarGridSpec(num...  15.5 us
    pallas_call x1, Pallas kernels, toeplitz(): pl.pallas_call(toeplitz_kernel, grid=(groups, blocks // WIDE), in_specs=[...  11.2 us
    ppermute x1, waiting for transfers between devices, on_device(): other = lax.ppermute(other, 'xh', [(0, 1), (1, 0)])  11.2 us
    ppermute x1, waiting for transfers between devices, on_device(): lax.ppermute(rim, CTX, [(i, (i + 1) % ctx_size) for i in range(ctx_size)])  8.96 us
  transfers between devices with their start and end apart: 9, of which 8 were waited for; matrix products, arithmetic and copies ran while one was open for 2% of the time, Pallas kernels for 21%

profile of v1, /device:TPU:1, one launch (start us, length us, event | category | flops | bytes accessed | tf_op | source)
XLA Modules:
  0.0 201.8 jit_solution(8180665262244825584)
XLA Ops:
  6.5 0.7 all-gather.2.cloned.1.call-update
  7.3 0.9 slice.15
  8.2 3.7 %collective-permute-start = (bf16[3,2,2048]{2,1,0:T(2,128)(2,1)S(1)}, bf16[3,2,2048]{2,1,0:T(2,128)(2,1)S(1)}, u32[]{:S(2)}, u32[]{:S(2)}) collective-permute-start(bf16[3,2,2048]{2,1,0:T(2,128)(2,1)S(1)} %slice.15), channel_id=1, source_target_pairs={{0,4},{4,8},{8,12},{12,16},{16,20},{20,24},{24,28},{28,32},{32,36}... | collective-permute-start | bytes 73736 | tf_op jit(solution)/shard_map/ppermute | solution.py:194
  11.8 9.0 %collective-permute-done.halo_ref = bf16[3,2,2048]{2,1,0:T(2,128)(2,1)S(1)} collective-permute-done((bf16[3,2,2048]{2,1,0:T(2,128)(2,1)S(1)}, bf16[3,2,2048]{2,1,0:T(2,128)(2,1)S(1)}, u32[]{:S(2)}, u32[]{:S(2)}) %collective-permute-start) | collective-permute-done | bytes 24608 | tf_op jit(solution)/shard_map/ppermute | solution.py:194
  20.8 0.6 copy-done.5
  21.4 7.2 %featurize.1 = (bf16[2048,256]{1,0:T(8,128)(2,1)}, bf16[2048,256]{1,0:T(8,128)(2,1)}) custom-call(s32[1]{0:T(128)} %bitcast.first_ref, bf16[3,256,2048]{2,1,0:T(8,128)(2,1)} %x_ref.1, bf16[3,2,2048]{2,1,0:T(2,128)(2,1)} %copy-done.5, f32[3,3,2048]{2,1,0:T(4,128)} %w_ref.1), custom_call_target="tpu_custom_call" | custom-call | tf_op jit(solution)/shard_map/featurize/pallas_call | solution.py:38
  28.6 6.7 %all-to-all-start = ((bf16[64,32,256]{2,1,0:T(8,128)(2,1)}), bf16[64,32,256]{2,1,0:T(8,128)(2,1)S(1)}, u32[]{:S(2)}, u32[]{:S(2)}) async-start(bf16[64,32,256]{2,1,0:T(8,128)(2,1)} %bitcast.19), calls=%async_computation | async-start | bytes 2097152 | tf_op jit(solution)/shard_map/all_to_all | solution.py:199
  35.4 0.7 broadcast_in_dim.7.h_ref
  36.1 11.2 %toeplitz.1.t_ref = bf16[2,64,256,256]{3,2,1,0:T(8,128)(2,1)} custom-call(f32[2,1,16640]{2,1,0:T(1,128)} %broadcast_in_dim.7.h_ref), custom_call_target="tpu_custom_call" | custom-call | bytes 50331648 | tf_op jit(solution)/shard_map/toeplitz/pallas_call | solution.py:71
  47.4 21.6 %all-to-all-done.x_ref = bf16[64,32,256]{2,1,0:T(8,128)(2,1)S(1)} async-done(((bf16[64,32,256]{2,1,0:T(8,128)(2,1)}), bf16[64,32,256]{2,1,0:T(8,128)(2,1)S(1)}, u32[]{:S(2)}, u32[]{:S(2)}) %all-to-all-start) | async-done | bytes 1048608 | tf_op jit(solution)/shard_map/all_to_all | solution.py:199
  68.9 1.0 copy-done.2
  69.9 20.5 %long_conv.1 = bf16[64,32,256]{2,1,0:T(8,128)(2,1)} custom-call(bf16[64,32,256]{2,1,0:T(8,128)(2,1)} %copy-done.2, bf16[2,64,256,256]{3,2,1,0:T(8,128)(2,1)} %toeplitz.1.t_ref), custom_call_target="tpu_custom_call" | custom-call | flops 8589934592 | bytes 20971520 | tf_op jit(solution)/shard_map/long_conv/pallas_call | solution.py:117
  90.4 7.3 %all-to-all-start.1 = ((bf16[32,2,32,256]{3,2,1,0:T(8,128)(2,1)}), bf16[32,2,32,256]{3,2,1,0:T(8,128)(2,1)S(1)}, u32[]{:S(2)}, u32[]{:S(2)}) async-start(bf16[32,2,32,256]{3,2,1,0:T(8,128)(2,1)} %bitcast.18), calls=%async_computation.1 | async-start | bytes 2097152 | tf_op jit(solution)/shard_map/all_to_all | solution.py:212
  97.8 0.9 collective-permute-start.1
  98.7 0.6 pad_add_fusion
  99.3 11.2 %collective-permute-done.1 = bf16[32,32,256]{2,1,0:T(8,128)(2,1)S(1)} collective-permute-done((bf16[32,32,256]{2,1,0:T(8,128)(2,1)S(1)}, bf16[32,32,256]{2,1,0:T(8,128)(2,1)S(1)}, u32[]{:S(2)}, u32[]{:S(2)}) %collective-permute-start.1) | collective-permute-done | bytes 524320 | tf_op jit(solution)/shard_map/ppermute | solution.py:207
  110.5 1.1 maximum_select_fusion.gate_ref
  111.7 25.0 %all-to-all-done.1.conv_ref = bf16[32,2,32,256]{3,2,1,0:T(8,128)(2,1)S(1)} async-done(((bf16[32,2,32,256]{3,2,1,0:T(8,128)(2,1)}), bf16[32,2,32,256]{3,2,1,0:T(8,128)(2,1)S(1)}, u32[]{:S(2)}, u32[]{:S(2)}) %all-to-all-start.1) | async-done | bytes 1048608 | tf_op jit(solution)/shard_map/all_to_all | solution.py:212
  136.7 1.0 copy-done
  137.7 3.8 %gating.1.a_ref = bf16[2,256,1024]{2,1,0:T(8,128)(2,1)} custom-call(bf16[32,2,32,256]{3,2,1,0:T(8,128)(2,1)} %copy-done, bf16[32,2,32,256]{3,2,1,0:T(8,128)(2,1)} %maximum_select_fusion.gate_ref), custom_call_target="tpu_custom_call" | custom-call | tf_op jit(solution)/shard_map/gating/pallas_call | solution.py:149
  141.8 7.6 %project.2 = bf16[4,256,1024]{2,1,0:T(8,128)(2,1)} custom-call(s32[2,4]{1,0:T(2,128)} %get-tuple-element.14.where_ref, bf16[2,256,1024]{2,1,0:T(8,128)(2,1)} %gating.1.a_ref, bf16[1024,4096]{1,0:T(8,128)(2,1)} %all-gather.2.cloned.1.call-done.w_ref), custom_call_target="tpu_custom_call" | custom-call | tf_op jit(solution)/shard_map/project/pallas_call | solution.py:172
  149.4 2.8 %collective-permute-start.2 = (bf16[4,256,1024]{2,1,0:T(8,128)(2,1)}, bf16[4,256,1024]{2,1,0:T(8,128)(2,1)S(1)}, u32[]{:S(2)}, u32[]{:S(2)}) collective-permute-start(bf16[4,256,1024]{2,1,0:T(8,128)(2,1)} %project.2), channel_id=1, source_target_pairs={{0,1},{1,0},{2,3},{3,2},{4,5},{5,4},{6,7},{7,6},{8,9},{9,8},{10,11... | collective-permute-start | bytes 6291464 | tf_op jit(solution)/shard_map/ppermute | solution.py:221
  152.1 4.0 %collective-permute-done.2.refs_0_ = bf16[4,256,1024]{2,1,0:T(8,128)(2,1)S(1)} collective-permute-done((bf16[4,256,1024]{2,1,0:T(8,128)(2,1)}, bf16[4,256,1024]{2,1,0:T(8,128)(2,1)S(1)}, u32[]{:S(2)}, u32[]{:S(2)}) %collective-permute-start.2) | collective-permute-done | bytes 2097184 | tf_op jit(solution)/shard_map/ppermute | solution.py:221
  156.1 1.3 copy-done.1
  157.5 7.9 %project.3 = bf16[4,256,1024]{2,1,0:T(8,128)(2,1)} custom-call(s32[2,4]{1,0:T(2,128)} %get-tuple-element.15.where_ref, bf16[2,256,1024]{2,1,0:T(8,128)(2,1)} %gating.1.a_ref, bf16[1024,4096]{1,0:T(8,128)(2,1)} %all-gather.2.cloned.1.call-done.w_ref, bf16[4,256,1024]{2,1,0:T(8,128)(2,1)} %copy-done.1), custom_call_target="tpu_custom_call" | custom-call | tf_op jit(solution)/shard_map/project/pallas_call | solution.py:172
  165.4 1.5 slice_bitcast_fusion.2
  166.8 0.6 collective-permute-start.3
  167.5 1.1 collective-permute-start.4
  168.6 1.4 collective-permute-start.5
  170.0 22.5 %collective-permute-done.3 = bf16[256,1024]{1,0:T(8,128)(2,1)S(1)} collective-permute-done((bf16[256,1024]{1,0:T(8,128)(2,1)S(1)}, bf16[256,1024]{1,0:T(8,128)(2,1)S(1)}, u32[]{:S(2)}, u32[]{:S(2)}) %collective-permute-start.3) | collective-permute-done | bytes 524320 | tf_op jit(solution)/shard_map/ppermute | solution.py:225
  192.5 0.3 collective-permute-done.5
  192.8 2.2 %fusion.2 = bf16[256,1024]{1,0:T(8,128)(2,1)} fusion(bf16[256,1024]{1,0:T(8,128)(2,1)S(1)} %collective-permute-done.5, bf16[256,1024]{1,0:T(8,128)(2,1)S(1)} %collective-permute-done.4, bf16[256,1024]{1,0:T(8,128)(2,1)S(1)} %collective-permute-done.3, bf16[4,256,1024]{2,1,0:T(8,128)(2,1)} %project.3), kind=kLoop, calls=%fused_computation.4 | loop fusion | flops 2097152 | bytes 2621440 | tf_op jit(solution)/shard_map/convert_element_type | solution.py:227
  (15 shorter events, 0.5 us)
Async XLA Ops:
  6.5 135.2 %all-gather.2.cloned.1.call-start = ((), (), s32[]{:S(2)}) async-start(), calls=%async_computation.2 | async-start | bytes 8650752 | tf_op jit(solution)/shard_map/all_gather | solution.py:196
  8.2 12.6 %collective-permute-start = (bf16[3,2,2048]{2,1,0:T(2,128)(2,1)S(1)}, bf16[3,2,2048]{2,1,0:T(2,128)(2,1)S(1)}, u32[]{:S(2)}, u32[]{:S(2)}) collective-permute-start(bf16[3,2,2048]{2,1,0:T(2,128)(2,1)S(1)} %slice.15), channel_id=1, source_target_pairs={{0,4},{4,8},{8,12},{12,16},{16,20},{20,24},{24,28},{28,32},{32,36}... | collective-permute-start | bytes 73736 | tf_op jit(solution)/shard_map/ppermute | solution.py:194
  20.8 0.6 copy-start.5
  21.4 13.9 %copy-start.4 = (f32[2,16384]{1,0:T(2,128)S(1)}, f32[2,16384]{1,0:T(2,128)}, u32[]{:S(2)}) copy-start(f32[2,16384]{1,0:T(2,128)} %param.6) | copy-start | bytes 393220
  28.6 40.3 %all-to-all-start = ((bf16[64,32,256]{2,1,0:T(8,128)(2,1)}), bf16[64,32,256]{2,1,0:T(8,128)(2,1)S(1)}, u32[]{:S(2)}, u32[]{:S(2)}) async-start(bf16[64,32,256]{2,1,0:T(8,128)(2,1)} %bitcast.19), calls=%async_computation | async-start | bytes 2097152 | tf_op jit(solution)/shard_map/all_to_all | solution.py:199
  68.9 1.0 copy-start.2
  90.4 7.3 %copy-start.3 = (bf16[2048,256]{1,0:T(8,128)(2,1)S(1)}, bf16[2048,256]{1,0:T(8,128)(2,1)}, u32[]{:S(2)}) copy-start(bf16[2048,256]{1,0:T(8,128)(2,1)} %get-tuple-element.8) | copy-start | bytes 3145732
  90.4 46.2 %all-to-all-start.1 = ((bf16[32,2,32,256]{3,2,1,0:T(8,128)(2,1)}), bf16[32,2,32,256]{3,2,1,0:T(8,128)(2,1)S(1)}, u32[]{:S(2)}, u32[]{:S(2)}) async-start(bf16[32,2,32,256]{3,2,1,0:T(8,128)(2,1)} %bitcast.18), calls=%async_computation.1 | async-start | bytes 2097152 | tf_op jit(solution)/shard_map/all_to_all | solution.py:212
  97.8 12.7 %collective-permute-start.1 = (bf16[32,32,256]{2,1,0:T(8,128)(2,1)S(1)}, bf16[32,32,256]{2,1,0:T(8,128)(2,1)S(1)}, u32[]{:S(2)}, u32[]{:S(2)}) collective-permute-start(bf16[32,32,256]{2,1,0:T(8,128)(2,1)S(1)} %get-tuple-element.13), channel_id=1, source_target_pairs={{0,4},{4,0},{1,5},{5,1},{2,6},{6,2},{3,7},{7,3},{8,12},{12,8},{9,1... | collective-permute-start | bytes 1572872 | tf_op jit(solution)/shard_map/ppermute | solution.py:207
  136.7 1.0 copy-start
  149.4 6.8 %collective-permute-start.2 = (bf16[4,256,1024]{2,1,0:T(8,128)(2,1)}, bf16[4,256,1024]{2,1,0:T(8,128)(2,1)S(1)}, u32[]{:S(2)}, u32[]{:S(2)}) collective-permute-start(bf16[4,256,1024]{2,1,0:T(8,128)(2,1)} %project.2), channel_id=1, source_target_pairs={{0,1},{1,0},{2,3},{3,2},{4,5},{5,4},{6,7},{7,6},{8,9},{9,8},{10,11... | collective-permute-start | bytes 6291464 | tf_op jit(solution)/shard_map/ppermute | solution.py:221
  156.1 1.3 copy-start.1
  166.8 25.7 %collective-permute-start.3 = (bf16[256,1024]{1,0:T(8,128)(2,1)S(1)}, bf16[256,1024]{1,0:T(8,128)(2,1)S(1)}, u32[]{:S(2)}, u32[]{:S(2)}) collective-permute-start(bf16[256,1024]{1,0:T(8,128)(2,1)S(1)} %get-tuple-element.9), channel_id=1, source_target_pairs={{0,2},{2,4},{4,6},{6,0},{1,3},{3,5},{5,7},{7,1},{8,10},{10,12},{12... | collective-permute-start | bytes 1572872 | tf_op jit(solution)/shard_map/ppermute | solution.py:225
  167.5 25.0 %collective-permute-start.4 = (bf16[256,1024]{1,0:T(8,128)(2,1)S(1)}, bf16[256,1024]{1,0:T(8,128)(2,1)S(1)}, u32[]{:S(2)}, u32[]{:S(2)}) collective-permute-start(bf16[256,1024]{1,0:T(8,128)(2,1)S(1)} %get-tuple-element.11), channel_id=1, source_target_pairs={{0,4},{2,6},{4,0},{6,2},{1,5},{3,7},{5,1},{7,3},{8,12},{10,14},{12... | collective-permute-start | bytes 1572872 | tf_op jit(solution)/shard_map/ppermute | solution.py:225
  168.6 24.2 %collective-permute-start.5 = (bf16[256,1024]{1,0:T(8,128)(2,1)S(1)}, bf16[256,1024]{1,0:T(8,128)(2,1)S(1)}, u32[]{:S(2)}, u32[]{:S(2)}) collective-permute-start(bf16[256,1024]{1,0:T(8,128)(2,1)S(1)} %get-tuple-element.10), channel_id=1, source_target_pairs={{0,6},{2,0},{4,2},{6,4},{1,7},{3,1},{5,3},{7,5},{8,14},{10,8},{12,... | collective-permute-start | bytes 1572872 | tf_op jit(solution)/shard_map/ppermute | solution.py:225
Sparse Core Ops, SparseCore 0:
  9.9 131.7 all-gather.1

commit v2 on v1

v2 whole, which is shorter than its diff:
```python
import functools

import jax
import jax.numpy as jnp
from jax import lax
from jax.experimental import pallas as pl
from jax.experimental.pallas import tpu as pltpu
from jax.sharding import Mesh, PartitionSpec as P

CTX = ("z", "y", "xh")
RING = ("xh", "xl")
F32, BF16 = jnp.float32, jnp.bfloat16
TOK = 256
WIDE = 8


VM = pl.BlockSpec(memory_space=pltpu.VMEM)
SM = pl.BlockSpec(memory_space=pltpu.SMEM)
MIB = 1024 * 1024


def params(mib):
    return pltpu.CompilerParams(vmem_limit_bytes=mib * MIB)


def featurize_kernel(width, x_ref, w_ref, prod_ref, gate_ref, edge_ref):
    tok, chans = x_ref.shape[1:]
    edge_ref[...] = x_ref[:, 0:8, :].astype(F32)

    def one(i, at):
        x = x_ref[i, :, at].astype(F32)
        x1 = pltpu.roll(x, 1, 0)
        x2 = pltpu.roll(x, 2, 0)
        taps = w_ref[i, :, at]
        mix = x2 * taps[0:1] + x1 * taps[1:2] + x * taps[2:3]
        return mix.astype(BF16).astype(F32)

    for c in range(chans // width):
        at = slice(c * width, (c + 1) * width)
        prod_ref[at, :] = (one(1, at) * one(2, at)).T.astype(BF16)
        gate_ref[at, :] = one(0, at).T.astype(BF16)


def featurize(features, taps):
    _, tok, chans = features.shape
    out = jax.ShapeDtypeStruct((chans, tok), BF16)
    return pl.pallas_call(
        functools.partial(featurize_kernel, 256),
        in_specs=[VM, VM],
        out_specs=[VM, VM, VM],
        out_shape=[out, out, jax.ShapeDtypeStruct((3, 8, chans), F32)],
        compiler_params=params(16),
        cost_estimate=pl.CostEstimate(flops=20 * MIB, bytes_accessed=8 * MIB, transcendentals=0),
        name="featurize",
    )(features, taps)


def join_kernel(live_ref, prod_in, gate_in, edge_ref, halo_ref, w_ref, prod_ref, gate_ref):
    live = live_ref[0] != 0
    lanes = 128
    chans = edge_ref.shape[2]
    lane = lax.broadcasted_iota(jnp.int32, (chans, lanes), 1)
    fresh = []
    for i in range(3):
        halo = jnp.where(live, halo_ref[i].astype(F32), 0.0)
        taps, edge = w_ref[i], edge_ref[i]
        row0 = halo[0:1] * taps[0:1] + halo[1:2] * taps[1:2] + edge[0:1] * taps[2:3]
        row1 = halo[1:2] * taps[0:1] + edge[0:1] * taps[1:2] + edge[1:2] * taps[2:3]
        fresh.append(jnp.concatenate([row0, row1], 0).astype(BF16).astype(F32))
    blank = jnp.zeros((lanes - 2, chans), F32)
    for value, old, new in ((fresh[1] * fresh[2], prod_in, prod_ref), (fresh[0], gate_in, gate_ref)):
        first = jnp.concatenate([value, blank], 0).T
        new[:, 0:lanes] = jnp.where(lane < 2, first, old[:, 0:lanes].astype(F32)).astype(BF16)
        new[:, lanes:] = old[:, lanes:]


def join(live, product, gate, edge, halo, taps):
    return pl.pallas_call(
        join_kernel,
        in_specs=[SM] + [VM] * 5,
        out_specs=[VM, VM],
        out_shape=[jax.ShapeDtypeStruct(x.shape, x.dtype) for x in (product, gate)],
        compiler_params=params(8),
        name="join",
    )(live, product, gate, edge, halo, taps)


def toeplitz_kernel(h_ref, t_ref):
    groups, blocks = t_ref.shape[:2]
    span, strip = TOK * WIDE, 16

    def chunk(n, carry):
        g, s = n // (blocks // WIDE), n % (blocks // WIDE)
        lags = h_ref[g, :, pl.ds(pl.multiple_of(s * span, span), span + TOK)]
        wide = jnp.broadcast_to(lags, (strip, span + TOK))
        for i in range(TOK // strip):
            slid = pltpu.roll(wide, i * strip, 1, stride=1, stride_axis=0).astype(BF16)
            for k in range(WIDE):
                t_ref[g, s * WIDE + k, i * strip : (i + 1) * strip, :] = slid[:, (k + 1) * TOK : (k + 2) * TOK]
        return carry

    lax.fori_loop(0, groups * (blocks // WIDE), chunk, 0)


def toeplitz(filters):
    groups, _, length = filters.shape
    blocks = length // TOK - 1
    return pl.pallas_call(
        toeplitz_kernel,
        in_specs=[VM],
        out_specs=VM,
        out_shape=jax.ShapeDtypeStruct((groups, blocks, TOK, TOK), BF16),
        compiler_params=params(8),
        cost_estimate=pl.CostEstimate(flops=0, bytes_accessed=36 * MIB, transcendentals=0),
        name="toeplitz",
    )(filters)


def conv_kernel(x_ref, t_ref, y_ref, wide_ref, acc_ref):
    blocks = x_ref.shape[0]
    groups = t_ref.shape[0]
    per_group = x_ref.shape[1] // groups
    rows = blocks * per_group
    for g in range(groups):
        own = slice(g * per_group, (g + 1) * per_group)
        x = x_ref[:, own, :].reshape(rows, TOK)
        for j in range(WIDE):
            lead = j * per_group
            if lead:
                wide_ref[0:lead, j * TOK : (j + 1) * TOK] = jnp.zeros((lead, TOK), BF16)
            wide_ref[lead:, j * TOK : (j + 1) * TOK] = x[: rows - lead]
        for s in range(blocks // WIDE):
            lead = s * WIDE * per_group
            t = t_ref[g, s * WIDE : (s + 1) * WIDE].reshape(WIDE * TOK, TOK)
            part = jnp.dot(wide_ref[0 : rows - lead, :], t, preferred_element_type=F32)
            if s == 0:
                acc_ref[...] = part
            else:
                acc_ref[lead:, :] += part
        y_ref[:, own, :] = acc_ref[...].astype(BF16).reshape(blocks, per_group, TOK)


def long_conv(x, t):
    blocks, chans, tok = x.shape
    per_group = chans // t.shape[0]
    return pl.pallas_call(
        conv_kernel,
        in_specs=[VM, VM],
        out_specs=VM,
        out_shape=jax.ShapeDtypeStruct(x.shape, BF16),
        scratch_shapes=[
            pltpu.VMEM((blocks * per_group, WIDE * TOK), BF16),
            pltpu.VMEM((blocks * per_group, TOK), F32),
        ],
        compiler_params=params(14),
        cost_estimate=pl.CostEstimate(
            flops=chans * blocks * blocks * tok * tok, bytes_accessed=20 * MIB, transcendentals=0
        ),
        name="long_conv",
    )(x, t)


def gate_kernel(half_ref, conv_ref, near_ref, far_ref, out_ref):
    srcs, _, chans, tok = conv_ref.shape
    group = 8
    half = half_ref[0]
    for r in range(2):
        for c in range(srcs // group):
            some = slice(c * group, (c + 1) * group)
            conv = conv_ref[some, half if r == 0 else 1 - half].astype(F32)
            gate = near_ref[some, half] if r == 0 else far_ref[some]
            gated = (conv * gate.astype(F32)).astype(BF16).astype(F32)
            gated = gated.reshape(group * chans, tok).T.astype(BF16)
            out_ref[r * tok : (r + 1) * tok, c * group * chans : (c + 1) * group * chans] = gated


def gating(half, conv, near, far):
    srcs, halves, chans, tok = conv.shape
    return pl.pallas_call(
        gate_kernel,
        in_specs=[SM, VM, VM, VM],
        out_specs=VM,
        out_shape=jax.ShapeDtypeStruct((halves * tok, srcs * chans), BF16),
        compiler_params=params(8),
        name="gating",
    )(half, conv, near, far)


def project_kernel(own_ref, other_ref, w_ref, out_ref, acc_ref):
    step = pl.program_id(0)
    srcs, _, _, deep, width = w_ref.shape
    w = w_ref[...].reshape(srcs, 2, deep, width)
    part = jnp.dot(own_ref[...], w[:, 0].reshape(srcs * deep, width), preferred_element_type=F32)
    part += jnp.dot(other_ref[...], w[:, 1].reshape(srcs * deep, width), preferred_element_type=F32)

    @pl.when(step == 0)
    def _():
        acc_ref[...] = part

    @pl.when(step != 0)
    def _():
        acc_ref[...] += part

    @pl.when(step == pl.num_programs(0) - 1)
    def _():
        out_ref[...] = acc_ref[...].astype(BF16)


def project(lane, own, other, weights):
    tok, chans = own.shape
    srcs, _, _, deep, width = weights.shape
    steps = 2
    many = srcs // steps
    side = pl.BlockSpec((tok, many * deep), lambda s: (0, s))
    return pl.pallas_call(
        project_kernel,
        grid=(steps,),
        in_specs=[side, side, pl.BlockSpec((many, 1, 2, deep, width), lambda s: (s, lane, 0, 0, 0))],
        out_specs=pl.BlockSpec((tok, width), lambda s: (0, 0)),
        out_shape=jax.ShapeDtypeStruct((tok, width), BF16),
        scratch_shapes=[pltpu.VMEM((tok, width), F32)],
        compiler_params=params(24),
        name="project",
    )(own, other, weights)


def swap(x, axis):
    return lax.ppermute(x, axis, [(0, 1), (1, 0)])


def on_device(features, short_weight, filters, out_weight):
    tok, chans = features.shape[1:]
    deep, wide = out_weight.shape
    xh, xl, core = lax.axis_index("xh"), lax.axis_index("xl"), lax.axis_index("core")
    pick = functools.partial(lax.dynamic_index_in_dim, keepdims=False)

    def columns(lane, core):
        return lax.dynamic_slice_in_dim(out_weight, (lane * 2 + core) * (wide // 4), wide // 4, 1)

    given = swap(jnp.stack([columns(xl, 1 - core), columns(1 - xl, 1 - core)]), "core")
    rows = jnp.stack([columns(xl, core), given[0], columns(1 - xl, core), given[1]])
    weights = lax.all_gather(rows.reshape(2, 2, deep, wide // 4), ("z", "y"), axis=0)

    rim = features[:, tok - 2 :, :]
    ctx_size = lax.axis_size(CTX)
    halo = lax.ppermute(rim, CTX, [(i, (i + 1) % ctx_size) for i in range(ctx_size)])
    live = jnp.where(lax.axis_index(CTX) == 0, 0, 1).astype(jnp.int32)[None]
    product, gate, edge = featurize(features, short_weight)
    product, gate = join(live, product, gate, edge, halo, short_weight)
    mine = chans // ctx_size
    series = lax.all_to_all(
        product.reshape(ctx_size, mine, tok), CTX, split_axis=0, concat_axis=0, tiled=True
    )
    padded = jnp.pad(filters, ((0, 0), (TOK, 0)))[:, None, :]
    gate = gate.reshape(ctx_size // 2, 2, mine, tok)
    far_gate = swap(pick(gate, 1 - xh, 1), "xh")

    series, padded, far_gate = lax.optimization_barrier((series, padded, far_gate))
    convolved = long_conv(series, toeplitz(padded))
    convolved = convolved.reshape(ctx_size // 2, 2, mine, tok)
    back = lax.all_to_all(convolved, ("z", "y"), split_axis=0, concat_axis=0, tiled=True)
    own = gating(xh.astype(jnp.int32)[None], back, gate, far_gate)
    other = swap(own, "core")

    flat = [(0, 1), (1, 0), (2, 3), (3, 2)]
    cross = [(0, 3), (3, 0), (1, 2), (2, 1)]
    mid = tok // 2
    ends = project(0, own, other, weights)
    up = lax.ppermute(ends[tok : tok + mid], RING, flat)
    down = lax.ppermute(ends[tok + mid :], RING, cross)
    sides = project(1, own, other, weights)
    flat_near = lax.ppermute(sides[:mid], RING, flat)
    cross_near = lax.ppermute(sides[tok + mid :], RING, cross)
    flat_far = (sides[mid:tok].astype(F32) + down.astype(F32)).astype(BF16)
    cross_far = (sides[tok : tok + mid].astype(F32) + up.astype(F32)).astype(BF16)
    flat_far = lax.ppermute(flat_far, RING, flat)
    cross_far = lax.ppermute(cross_far, RING, cross)
    total = ends[:tok].astype(F32)
    total = total + jnp.concatenate([flat_near, flat_far]).astype(F32)
    total = total + jnp.concatenate([cross_far, cross_near]).astype(F32)
    return total.astype(BF16)


def solution(mesh):
    fine = Mesh(mesh.devices.reshape(8, 4, 2, 2, 2), ("z", "y", "xh", "xl", "core"))
    tp = ("xl", "core")
    in_specs = (
        P(None, CTX, tp),
        P(None, None, tp),
        P(tp + CTX, None),
        P(tp + CTX, None),
    )
    return jax.shard_map(
        on_device, mesh=fine, in_specs=in_specs, out_specs=P(CTX, tp), check_vma=False
    )
```

time: 203 us -> 178 us (0.88)
  blocking collectives: 0 us -> 44.3 us
  waiting for transfers between devices: 94.5 us -> 59.1 us
  Pallas kernels: 58.2 us -> 25.2 us
    all_to_all x0 -> x1, blocking collectives: none -> 44.3 us  [on_device(): lax.all_to_all(convolved, ('z', 'y'), split_axis=0, concat_axis=0, tiled=...]
    pallas_call x6 -> x7, Pallas kernels: 58.2 us -> 25.2 us  [the longest x1 9.88 us: long_conv(): pl.pallas_call(conv_kernel, in_specs=[VM, VM], out_specs=VM, out_shape=ja...]
    all_to_all x1 -> x0, waiting for transfers between devices: 25 us -> none  [on_device(): lax.all_to_all(convolved, ('z', 'y'), split_axis=0, concat_axis=0, tiled=...]
    all_gather x1, waiting for transfers between devices: 0.28 us -> 8.76 us  [on_device(): lax.all_gather(rows.reshape(2, 2, deep, wide // 4), ('z', 'y'), axis=0)]
    ppermute x5 -> x9, starting transfers between devices: 6.81 us -> 15.3 us  [the longest x3 9.24 us: swap(): return lax.ppermute(x, axis, [(0, 1), (1, 0)])]
    all_to_all x1 -> x0, starting transfers between devices: 7.26 us -> none  [on_device(): lax.all_to_all(convolved, ('z', 'y'), split_axis=0, concat_axis=0, tiled=...]
    all_to_all x1, waiting for transfers between devices: 21.6 us -> 15 us  [on_device(): lax.all_to_all(product.reshape(ctx_size, mine, tok), CTX, split_axis=0, c...]
    ppermute x5 -> x9, waiting for transfers between devices: 38 us -> 31.9 us  [the longest x3 20.9 us: swap(): return lax.ppermute(x, axis, [(0, 1), (1, 0)])]
  transfers between devices with their start and end apart: 9 -> 12, of which waited for: 8 -> 10; matrix products, arithmetic and copies ran while one was open for 2% -> 1% of each run, Pallas kernels for 21% -> 12%
where the time goes in v2:
time: 178 us
  waiting for transfers between devices  59.1 us (33%)
  blocking collectives  44.3 us (25%)
  starting transfers between devices  25.4 us (14%)
  Pallas kernels  25.2 us (14%)
  between operations  13.5 us (8%)
  local copies, waits for them, and re-layouts  8.34 us (5%)
  other arithmetic  2 us (1%)
    all_to_all x1, blocking collectives, on_device(): lax.all_to_all(convolved, ('z', 'y'), split_axis=0, concat_axis=0, tiled=...  44.3 us
    ppermute x3, waiting for transfers between devices, swap(): return lax.ppermute(x, axis, [(0, 1), (1, 0)])  20.9 us
    all_to_all x1, waiting for transfers between devices, on_device(): lax.all_to_all(product.reshape(ctx_size, mine, tok), CTX, split_axis=0, c...  15 us
    pallas_call x1, Pallas kernels, long_conv(): pl.pallas_call(conv_kernel, in_specs=[VM, VM], out_specs=VM, out_shape=ja...  9.88 us
    ppermute x3, starting transfers between devices, swap(): return lax.ppermute(x, axis, [(0, 1), (1, 0)])  9.24 us
    all_to_all x1, starting transfers between devices, on_device(): lax.all_to_all(product.reshape(ctx_size, mine, tok), CTX, split_axis=0, c...  9.06 us
    all_gather x1, waiting for transfers between devices, on_device(): lax.all_gather(rows.reshape(2, 2, deep, wide // 4), ('z', 'y'), axis=0)  8.76 us
    pallas_call x2, Pallas kernels, project(): pl.pallas_call(project_kernel, grid=(steps,), in_specs=[side, side, pl.Bl...  6.67 us
  transfers between devices with their start and end apart: 12, of which 10 were waited for; matrix products, arithmetic and copies ran while one was open for 1% of the time, Pallas kernels for 12%

profile of v2, /device:TPU:1, one launch (start us, length us, event | category | flops | bytes accessed | tf_op | source)
XLA Modules:
  0.0 177.9 jit_solution(4381166406491318202)
XLA Ops:
  6.5 1.0 dynamic-slice_bitcast_fusion.4
  7.6 3.3 %collective-permute-start.3 = (bf16[2,32,1024]{2,1,0:T(8,128)(2,1)S(1)}, bf16[2,32,1024]{2,1,0:T(8,128)(2,1)S(1)}, u32[]{:S(2)}, u32[]{:S(2)}) collective-permute-start(bf16[2,32,1024]{2,1,0:T(8,128)(2,1)S(1)} %pad_maximum_fusion.1), channel_id=1, source_target_pairs={{0,1},{1,0},{2,3},{3,2},{4,5},{5,4},{6,7},{7,6},{8,9},{9,8},{10,11... | collective-permute-start | bytes 393224 | tf_op jit(solution)/shard_map/ppermute | solution.py:228
  10.9 1.0 collective-permute-done.3
  11.9 0.7 pad_maximum_fusion
  12.6 0.9 slice.30
  13.6 1.1 collective-permute-start
  14.7 1.9 %copy-done.1 = bf16[3,256,2048]{2,1,0:T(8,128)(2,1)S(1)} copy-done((bf16[3,256,2048]{2,1,0:T(8,128)(2,1)S(1)}, bf16[3,256,2048]{2,1,0:T(8,128)(2,1)}, u32[]{:S(2)}) %copy-start.1) | copy-done | bytes 3145752
  16.6 0.9 copy-done.2
  17.4 2.7 %featurize.1 = (bf16[2048,256]{1,0:T(8,128)(2,1)S(1)}, bf16[2048,256]{1,0:T(8,128)(2,1)S(1)}, f32[3,8,2048]{2,1,0:T(8,128)S(1)}) custom-call(bf16[3,256,2048]{2,1,0:T(8,128)(2,1)S(1)} %copy-done.1, f32[3,3,2048]{2,1,0:T(4,128)S(1)} %copy-done.2), custom_call_target="tpu_custom_call" | custom-call | flops 20971520 | bytes 8388608 | tf_op jit(solution)/shard_map/featurize/pallas_call | solution.py:47
  20.2 3.4 %collective-permute-done.halo_ref = bf16[3,2,2048]{2,1,0:T(2,128)(2,1)S(1)} collective-permute-done((bf16[3,2,2048]{2,1,0:T(2,128)(2,1)S(1)}, bf16[3,2,2048]{2,1,0:T(2,128)(2,1)S(1)}, u32[]{:S(2)}, u32[]{:S(2)}) %collective-permute-start) | collective-permute-done | bytes 24608 | tf_op jit(solution)/shard_map/ppermute | solution.py:246
  23.6 1.6 join.1
  25.2 9.1 %all-to-all-start = ((bf16[64,32,256]{2,1,0:T(8,128)(2,1)}), bf16[64,32,256]{2,1,0:T(8,128)(2,1)S(1)}, u32[]{:S(2)}, u32[]{:S(2)}) async-start(bf16[64,32,256]{2,1,0:T(8,128)(2,1)} %bitcast.2), calls=%async_computation | async-start | bytes 2097152 | tf_op jit(solution)/shard_map/all_to_all | solution.py:251
  34.4 2.8 %collective-permute-start.1 = (bf16[32,32,256]{2,1,0:T(8,128)(2,1)S(1)}, bf16[32,32,256]{2,1,0:T(8,128)(2,1)S(1)}, u32[]{:S(2)}, u32[]{:S(2)}) collective-permute-start(bf16[32,32,256]{2,1,0:T(8,128)(2,1)S(1)} %dynamic-slice_bitcast_fusion), channel_id=1, source_target_pairs={{0,4},{4,0},{1,5},{5,1},{2,6},{6,2},{3,7},{7,3},{8,12},{12,8},{9,1... | collective-permute-start | bytes 1572872 | tf_op jit(solution)/shard_map/ppermute | solution.py:228
  37.3 17.7 %collective-permute-done.1.far_ref = bf16[32,32,256]{2,1,0:T(8,128)(2,1)S(1)} collective-permute-done((bf16[32,32,256]{2,1,0:T(8,128)(2,1)S(1)}, bf16[32,32,256]{2,1,0:T(8,128)(2,1)S(1)}, u32[]{:S(2)}, u32[]{:S(2)}) %collective-permute-start.1) | collective-permute-done | bytes 524320 | tf_op jit(solution)/shard_map/ppermute | solution.py:228
  55.0 15.0 %all-to-all-done.x_ref = bf16[64,32,256]{2,1,0:T(8,128)(2,1)S(1)} async-done(((bf16[64,32,256]{2,1,0:T(8,128)(2,1)}), bf16[64,32,256]{2,1,0:T(8,128)(2,1)S(1)}, u32[]{:S(2)}, u32[]{:S(2)}) %all-to-all-start) | async-done | bytes 1048608 | tf_op jit(solution)/shard_map/all_to_all | solution.py:251
  69.9 3.9 %toeplitz.1.t_ref = bf16[2,64,256,256]{3,2,1,0:T(8,128)(2,1)S(1)} custom-call(f32[2,1,16640]{2,1,0:T(1,128)S(1)} %broadcast_in_dim.11.h_ref), custom_call_target="tpu_custom_call" | custom-call | bytes 37748736 | tf_op jit(solution)/shard_map/toeplitz/pallas_call | solution.py:108
  73.8 9.9 %long_conv.1 = bf16[64,32,256]{2,1,0:T(8,128)(2,1)S(1)} custom-call(bf16[64,32,256]{2,1,0:T(8,128)(2,1)S(1)} %all-to-all-done.x_ref, bf16[2,64,256,256]{3,2,1,0:T(8,128)(2,1)S(1)} %toeplitz.1.t_ref), custom_call_target="tpu_custom_call" | custom-call | flops 8589934592 | bytes 20971520 | tf_op jit(solution)/shard_map/long_conv/pallas_call | solution.py:146
  83.7 44.3 %all_to_all.10.conv_ref = bf16[32,2,32,256]{3,2,1,0:T(8,128)(2,1)S(1)} all-to-all(bf16[32,2,32,256]{3,2,1,0:T(8,128)(2,1)S(1)} %bitcast.18), channel_id=1, replica_groups=mesh['z'=8,'y'=4,'xh'=2,'xl'=2,'core'=2] {'z','y'}, dimensions={0} | all-to-all | bytes 2097152 | tf_op jit(solution)/shard_map/all_to_all | solution.py:261
  128.4 3.1 %collective-permute-start.2 = (bf16[512,1024]{1,0:T(8,128)(2,1)S(1)}, bf16[512,1024]{1,0:T(8,128)(2,1)S(1)}, u32[]{:S(2)}, u32[]{:S(2)}) collective-permute-start(bf16[512,1024]{1,0:T(8,128)(2,1)S(1)} %gating.1.own_ref), channel_id=1, source_target_pairs={{0,1},{1,0},{2,3},{3,2},{4,5},{5,4},{6,7},{7,6},{8,9},{9,8},{10,11... | collective-permute-start | bytes 3145736 | tf_op jit(solution)/shard_map/ppermute | solution.py:228
  131.5 2.3 %collective-permute-done.2.other_ref = bf16[512,1024]{1,0:T(8,128)(2,1)S(1)} collective-permute-done((bf16[512,1024]{1,0:T(8,128)(2,1)S(1)}, bf16[512,1024]{1,0:T(8,128)(2,1)S(1)}, u32[]{:S(2)}, u32[]{:S(2)}) %collective-permute-start.2) | collective-permute-done | bytes 1048608 | tf_op jit(solution)/shard_map/ppermute | solution.py:228
  133.8 8.8 %all-gather.2.cloned.1.call-done.w_ref = bf16[32,2,2,32,1024]{4,3,2,1,0:T(8,128)(2,1)} async-done(((bf16[1,2,2,32,1024]{4,3,2,1,0:T(8,128)(2,1)}), bf16[32,2,2,32,1024]{4,3,2,1,0:T(8,128)(2,1)}) %all-gather.2.cloned.1.call-update) | async-done | bytes 8388624 | tf_op jit(solution)/shard_map/all_gather | solution.py:242
  142.6 3.4 %copy-done = bf16[32,2,2,32,1024]{4,3,2,1,0:T(8,128)(2,1)S(1)} copy-done((bf16[32,2,2,32,1024]{4,3,2,1,0:T(8,128)(2,1)S(1)}, bf16[32,2,2,32,1024]{4,3,2,1,0:T(8,128)(2,1)}, u32[]{:S(2)}) %copy-start) | copy-done | bytes 8388632
  146.0 3.3 %project.2 = bf16[512,1024]{1,0:T(8,128)(2,1)S(1)} custom-call(bf16[512,1024]{1,0:T(8,128)(2,1)S(1)} %gating.1.own_ref, bf16[512,1024]{1,0:T(8,128)(2,1)S(1)} %collective-permute-done.2.other_ref, bf16[32,2,2,32,1024]{4,3,2,1,0:T(8,128)(2,1)S(1)} %copy-done), custom_call_target="tpu_custom_call" | custom-call | tf_op jit(solution)/shard_map/project/pallas_call | solution.py:215
  149.4 2.6 %collective-permute-start.5 = (bf16[128,1024]{1,0:T(8,128)(2,1)S(1)}, bf16[128,1024]{1,0:T(8,128)(2,1)S(1)}, u32[]{:S(2)}, u32[]{:S(2)}) collective-permute-start(bf16[128,1024]{1,0:T(8,128)(2,1)S(1)} %get-tuple-element.24), channel_id=1, source_target_pairs={{0,6},{6,0},{2,4},{4,2},{1,7},{7,1},{3,5},{5,3},{8,14},{14,8},{10,... | collective-permute-start | bytes 786440 | tf_op jit(solution)/shard_map/ppermute | solution.py:270
  151.9 3.3 %project.3 = bf16[512,1024]{1,0:T(8,128)(2,1)S(1)} custom-call(bf16[512,1024]{1,0:T(8,128)(2,1)S(1)} %gating.1.own_ref, bf16[512,1024]{1,0:T(8,128)(2,1)S(1)} %collective-permute-done.2.other_ref, bf16[32,2,2,32,1024]{4,3,2,1,0:T(8,128)(2,1)S(1)} %copy-done), custom_call_target="tpu_custom_call" | custom-call | tf_op jit(solution)/shard_map/project/pallas_call | solution.py:215
  155.3 1.5 collective-permute-start.4
  157.1 1.6 collective-permute-done.7
  158.9 0.4 collective-permute-start.6
  159.4 1.3 collective-permute-start.8
  160.7 3.7 %collective-permute-done.4 = bf16[128,1024]{1,0:T(8,128)(2,1)S(1)} collective-permute-done((bf16[128,1024]{1,0:T(8,128)(2,1)S(1)}, bf16[128,1024]{1,0:T(8,128)(2,1)S(1)}, u32[]{:S(2)}, u32[]{:S(2)}) %collective-permute-start.4) | collective-permute-done | bytes 262176 | tf_op jit(solution)/shard_map/ppermute | solution.py:272
  164.4 5.6 %collective-permute-done.6 = bf16[128,1024]{1,0:T(8,128)(2,1)S(1)} collective-permute-done((bf16[128,1024]{1,0:T(8,128)(2,1)S(1)}, bf16[128,1024]{1,0:T(8,128)(2,1)S(1)}, u32[]{:S(2)}, u32[]{:S(2)}) %collective-permute-start.6) | collective-permute-done | bytes 262176 | tf_op jit(solution)/shard_map/ppermute | solution.py:276
  170.0 1.1 add_convert_fusion
  (21 shorter events, 1.2 us)
Async XLA Ops:
  6.5 30.6 %copy-start.3 = (f32[2,16384]{1,0:T(2,128)S(1)}, f32[2,16384]{1,0:T(2,128)}, u32[]{:S(2)}) copy-start(f32[2,16384]{1,0:T(2,128)} %param.6) | copy-start | bytes 393220
  6.5 136.1 %all-gather.2.cloned.1.call-start = ((), (), s32[]{:S(2)}) async-start(), calls=%async_computation.2 | async-start | bytes 8650752 | tf_op jit(solution)/shard_map/all_gather | solution.py:242
  7.6 4.3 %collective-permute-start.3 = (bf16[2,32,1024]{2,1,0:T(8,128)(2,1)S(1)}, bf16[2,32,1024]{2,1,0:T(8,128)(2,1)S(1)}, u32[]{:S(2)}, u32[]{:S(2)}) collective-permute-start(bf16[2,32,1024]{2,1,0:T(8,128)(2,1)S(1)} %pad_maximum_fusion.1), channel_id=1, source_target_pairs={{0,1},{1,0},{2,3},{3,2},{4,5},{5,4},{6,7},{7,6},{8,9},{9,8},{10,11... | collective-permute-start | bytes 393224 | tf_op jit(solution)/shard_map/ppermute | solution.py:228
  13.6 10.0 %collective-permute-start = (bf16[3,2,2048]{2,1,0:T(2,128)(2,1)S(1)}, bf16[3,2,2048]{2,1,0:T(2,128)(2,1)S(1)}, u32[]{:S(2)}, u32[]{:S(2)}) collective-permute-start(bf16[3,2,2048]{2,1,0:T(2,128)(2,1)S(1)} %slice.30), channel_id=1, source_target_pairs={{0,4},{4,8},{8,12},{12,16},{16,20},{20,24},{24,28},{28,32},{32,36}... | collective-permute-start | bytes 73736 | tf_op jit(solution)/shard_map/ppermute | solution.py:246
  14.7 1.9 %copy-start.1 = (bf16[3,256,2048]{2,1,0:T(8,128)(2,1)S(1)}, bf16[3,256,2048]{2,1,0:T(8,128)(2,1)}, u32[]{:S(2)}) copy-start(bf16[3,256,2048]{2,1,0:T(8,128)(2,1)} %x_ref.1) | copy-start | bytes 9437188
  16.5 0.9 copy-start.2
  25.2 44.7 %all-to-all-start = ((bf16[64,32,256]{2,1,0:T(8,128)(2,1)}), bf16[64,32,256]{2,1,0:T(8,128)(2,1)S(1)}, u32[]{:S(2)}, u32[]{:S(2)}) async-start(bf16[64,32,256]{2,1,0:T(8,128)(2,1)} %bitcast.2), calls=%async_computation | async-start | bytes 2097152 | tf_op jit(solution)/shard_map/all_to_all | solution.py:251
  34.4 20.6 %collective-permute-start.1 = (bf16[32,32,256]{2,1,0:T(8,128)(2,1)S(1)}, bf16[32,32,256]{2,1,0:T(8,128)(2,1)S(1)}, u32[]{:S(2)}, u32[]{:S(2)}) collective-permute-start(bf16[32,32,256]{2,1,0:T(8,128)(2,1)S(1)} %dynamic-slice_bitcast_fusion), channel_id=1, source_target_pairs={{0,4},{4,0},{1,5},{5,1},{2,6},{6,2},{3,7},{7,3},{8,12},{12,8},{9,1... | collective-permute-start | bytes 1572872 | tf_op jit(solution)/shard_map/ppermute | solution.py:228
  128.4 5.4 %collective-permute-start.2 = (bf16[512,1024]{1,0:T(8,128)(2,1)S(1)}, bf16[512,1024]{1,0:T(8,128)(2,1)S(1)}, u32[]{:S(2)}, u32[]{:S(2)}) collective-permute-start(bf16[512,1024]{1,0:T(8,128)(2,1)S(1)} %gating.1.own_ref), channel_id=1, source_target_pairs={{0,1},{1,0},{2,3},{3,2},{4,5},{5,4},{6,7},{7,6},{8,9},{9,8},{10,11... | collective-permute-start | bytes 3145736 | tf_op jit(solution)/shard_map/ppermute | solution.py:228
  142.6 3.4 %copy-start = (bf16[32,2,2,32,1024]{4,3,2,1,0:T(8,128)(2,1)S(1)}, bf16[32,2,2,32,1024]{4,3,2,1,0:T(8,128)(2,1)}, u32[]{:S(2)}) copy-start(bf16[32,2,2,32,1024]{4,3,2,1,0:T(8,128)(2,1)} %all-gather.2.cloned.1.call-done.w_ref) | copy-start | bytes 25165828
  149.4 7.8 %collective-permute-start.5 = (bf16[128,1024]{1,0:T(8,128)(2,1)S(1)}, bf16[128,1024]{1,0:T(8,128)(2,1)S(1)}, u32[]{:S(2)}, u32[]{:S(2)}) collective-permute-start(bf16[128,1024]{1,0:T(8,128)(2,1)S(1)} %get-tuple-element.24), channel_id=1, source_target_pairs={{0,6},{6,0},{2,4},{4,2},{1,7},{7,1},{3,5},{5,3},{8,14},{14,8},{10,... | collective-permute-start | bytes 786440 | tf_op jit(solution)/shard_map/ppermute | solution.py:270
  151.9 6.8 %collective-permute-start.7 = (bf16[128,1024]{1,0:T(8,128)(2,1)S(1)}, bf16[128,1024]{1,0:T(8,128)(2,1)S(1)}, u32[]{:S(2)}, u32[]{:S(2)}) collective-permute-start(bf16[128,1024]{1,0:T(8,128)(2,1)S(1)} %get-tuple-element.23), channel_id=1, source_target_pairs={{0,2},{2,0},{4,6},{6,4},{1,3},{3,1},{5,7},{7,5},{8,10},{10,8},{12,... | collective-permute-start | bytes 786440 | tf_op jit(solution)/shard_map/ppermute | solution.py:269
  155.3 9.0 %collective-permute-start.4 = (bf16[128,1024]{1,0:T(8,128)(2,1)S(1)}, bf16[128,1024]{1,0:T(8,128)(2,1)S(1)}, u32[]{:S(2)}, u32[]{:S(2)}) collective-permute-start(bf16[128,1024]{1,0:T(8,128)(2,1)S(1)} %get-tuple-element.26), channel_id=1, source_target_pairs={{0,2},{2,0},{4,6},{6,4},{1,3},{3,1},{5,7},{7,5},{8,10},{10,8},{12,... | collective-permute-start | bytes 786440 | tf_op jit(solution)/shard_map/ppermute | solution.py:272
  156.9 7.5 %collective-permute-start.9 = (bf16[128,1024]{1,0:T(8,128)(2,1)S(1)}, bf16[128,1024]{1,0:T(8,128)(2,1)S(1)}, u32[]{:S(2)}, u32[]{:S(2)}) collective-permute-start(bf16[128,1024]{1,0:T(8,128)(2,1)S(1)} %get-tuple-element.25), channel_id=1, source_target_pairs={{0,6},{6,0},{2,4},{4,2},{1,7},{7,1},{3,5},{5,3},{8,14},{14,8},{10,... | collective-permute-start | bytes 786440 | tf_op jit(solution)/shard_map/ppermute | solution.py:273
  158.9 11.0 %collective-permute-start.6 = (bf16[128,1024]{1,0:T(8,128)(2,1)S(1)}, bf16[128,1024]{1,0:T(8,128)(2,1)S(1)}, u32[]{:S(2)}, u32[]{:S(2)}) collective-permute-start(bf16[128,1024]{1,0:T(8,128)(2,1)S(1)} %get-tuple-element.22), channel_id=1, source_target_pairs={{0,2},{2,0},{4,6},{6,4},{1,3},{3,1},{5,7},{7,5},{8,10},{10,8},{12,... | collective-permute-start | bytes 786440 | tf_op jit(solution)/shard_map/ppermute | solution.py:276
  159.4 10.6 %collective-permute-start.8 = (bf16[128,1024]{1,0:T(8,128)(2,1)S(1)}, bf16[128,1024]{1,0:T(8,128)(2,1)S(1)}, u32[]{:S(2)}, u32[]{:S(2)}) collective-permute-start(bf16[128,1024]{1,0:T(8,128)(2,1)S(1)} %get-tuple-element.21), channel_id=1, source_target_pairs={{0,6},{6,0},{2,4},{4,2},{1,7},{7,1},{3,5},{5,3},{8,14},{14,8},{10,... | collective-permute-start | bytes 786440 | tf_op jit(solution)/shard_map/ppermute | solution.py:277
Sparse Core Ops, SparseCore 0:
  12.8 129.7 all-gather.1

commit v3 on v2

--- a/solution.py
+++ b/solution.py
@@ -186,40 +186,30 @@
     )(half, conv, near, far)
 
 
-def project_kernel(own_ref, other_ref, w_ref, out_ref, acc_ref):
-    step = pl.program_id(0)
+def project_kernel(rows, lane, own_ref, other_ref, w_ref, *out_refs):
     srcs, _, _, deep, width = w_ref.shape
-    w = w_ref[...].reshape(srcs, 2, deep, width)
-    part = jnp.dot(own_ref[...], w[:, 0].reshape(srcs * deep, width), preferred_element_type=F32)
-    part += jnp.dot(other_ref[...], w[:, 1].reshape(srcs * deep, width), preferred_element_type=F32)
-
-    @pl.when(step == 0)
-    def _():
-        acc_ref[...] = part
-
-    @pl.when(step != 0)
-    def _():
-        acc_ref[...] += part
-
-    @pl.when(step == pl.num_programs(0) - 1)
-    def _():
-        out_ref[...] = acc_ref[...].astype(BF16)
-
-
-def project(lane, own, other, weights):
-    tok, chans = own.shape
+    part = None
+    for c, side_ref in enumerate((own_ref, other_ref)):
+        w = w_ref[:, lane, c].reshape(srcs * deep, width)
+        term = jnp.dot(side_ref[rows, :], w, preferred_element_type=F32)
+        part = term if part is None else part + term
+    tall = out_refs[0].shape[0]
+    for n, out_ref in enumerate(out_refs):
+        out_ref[...] = part[n * tall : (n + 1) * tall].astype(out_ref.dtype)
+
+
+def project(rows, lane, pieces, own, other, weights, out_type=BF16):
     srcs, _, _, deep, width = weights.shape
-    steps = 2
-    many = srcs // steps
-    side = pl.BlockSpec((tok, many * deep), lambda s: (0, s))
-    return pl.pallas_call(
-        project_kernel,
-        grid=(steps,),
-        in_specs=[side, side, pl.BlockSpec((many, 1, 2, deep, width), lambda s: (s, lane, 0, 0, 0))],
-        out_specs=pl.BlockSpec((tok, width), lambda s: (0, 0)),
-        out_shape=jax.ShapeDtypeStruct((tok, width), BF16),
-        scratch_shapes=[pltpu.VMEM((tok, width), F32)],
-        compiler_params=params(24),
+    tok = rows.stop - rows.start
+    return pl.pallas_call(
+        functools.partial(project_kernel, rows, lane),
+        in_specs=[VM, VM, VM],
+        out_specs=[VM] * pieces,
+        out_shape=[jax.ShapeDtypeStruct((tok // pieces, width), out_type)] * pieces,
+        compiler_params=params(16),
+        cost_estimate=pl.CostEstimate(
+            flops=4 * tok * srcs * deep * width, bytes_accessed=6 * MIB, transcendentals=0
+        ),
         name="project",
     )(own, other, weights)
 
@@ -264,18 +254,18 @@
 
     flat = [(0, 1), (1, 0), (2, 3), (3, 2)]
     cross = [(0, 3), (3, 0), (1, 2), (2, 1)]
-    mid = tok // 2
-    ends = project(0, own, other, weights)
-    up = lax.ppermute(ends[tok : tok + mid], RING, flat)
-    down = lax.ppermute(ends[tok + mid :], RING, cross)
-    sides = project(1, own, other, weights)
-    flat_near = lax.ppermute(sides[:mid], RING, flat)
-    cross_near = lax.ppermute(sides[tok + mid :], RING, cross)
-    flat_far = (sides[mid:tok].astype(F32) + down.astype(F32)).astype(BF16)
-    cross_far = (sides[tok : tok + mid].astype(F32) + up.astype(F32)).astype(BF16)
+    whole = (own, other, weights)
+    ahead = project(slice(tok, 2 * tok), 0, 2, *whole)
+    up = lax.ppermute(ahead[0], RING, flat)
+    down = lax.ppermute(ahead[1], RING, cross)
+    sides = project(slice(0, 2 * tok), 1, 4, *whole)
+    flat_near = lax.ppermute(sides[0], RING, flat)
+    cross_near = lax.ppermute(sides[3], RING, cross)
+    flat_far = (sides[1].astype(F32) + down.astype(F32)).astype(BF16)
+    cross_far = (sides[2].astype(F32) + up.astype(F32)).astype(BF16)
     flat_far = lax.ppermute(flat_far, RING, flat)
     cross_far = lax.ppermute(cross_far, RING, cross)
-    total = ends[:tok].astype(F32)
+    (total,) = project(slice(0, tok), 0, 1, *whole, F32)
     total = total + jnp.concatenate([flat_near, flat_far]).astype(F32)
     total = total + jnp.concatenate([cross_far, cross_near]).astype(F32)
     return total.astype(BF16)

time: 178 us -> 177 us (level)
  Pallas kernels: 25.2 us -> 23.3 us
    ppermute x1, waiting for transfers between devices: 0.01 us -> 5.62 us  [on_device(): cross_far = lax.ppermute(cross_far, RING, cross)]
    ppermute x1, waiting for transfers between devices: 5.61 us -> 0.01 us  [on_device(): flat_far = lax.ppermute(flat_far, RING, flat)]
    pallas_call x2 -> x3, Pallas kernels: 6.67 us -> 4.81 us  [project(): pl.pallas_call(functools.partial(project_kernel, rows, lane), in_specs=[V...]
  transfers between devices with their start and end apart: 12 -> 12, of which waited for: 10 -> 10; matrix products, arithmetic and copies ran while one was open for 1% -> 1% of each run, Pallas kernels for 12% -> 13%
where the time goes in v3:
time: 177 us; the launch traced here: 176 us
  waiting for transfers between devices  58.5 us (33%)
  blocking collectives  44.4 us (25%)
  starting transfers between devices  26.4 us (15%)
  Pallas kernels  23.3 us (13%)
  between operations  13.5 us (8%)
  local copies, waits for them, and re-layouts  8.27 us (5%)
  other arithmetic  1.95 us (1%)
    all_to_all x1, blocking collectives, on_device(): lax.all_to_all(convolved, ('z', 'y'), split_axis=0, concat_axis=0, tiled=...  44.4 us
    ppermute x3, waiting for transfers between devices, swap(): return lax.ppermute(x, axis, [(0, 1), (1, 0)])  21 us
    all_to_all x1, waiting for transfers between devices, on_device(): lax.all_to_all(product.reshape(ctx_size, mine, tok), CTX, split_axis=0, c...  15 us
    pallas_call x1, Pallas kernels, long_conv(): pl.pallas_call(conv_kernel, in_specs=[VM, VM], out_specs=VM, out_shape=ja...  9.88 us
    ppermute x3, starting transfers between devices, swap(): return lax.ppermute(x, axis, [(0, 1), (1, 0)])  9.2 us
    all_gather x1, waiting for transfers between devices, on_device(): lax.all_gather(rows.reshape(2, 2, deep, wide // 4), ('z', 'y'), axis=0)  9.13 us
    all_to_all x1, starting transfers between devices, on_device(): lax.all_to_all(product.reshape(ctx_size, mine, tok), CTX, split_axis=0, c...  9.06 us
    unnamed x8, local copies, waits for them, and re-layouts  6.17 us
  transfers between devices with their start and end apart: 12, of which 10 were waited for; matrix products, arithmetic and copies ran while one was open for 1% of the time, Pallas kernels for 13%

profile of v3, /device:TPU:1, one launch (start us, length us, event | category | flops | bytes accessed | tf_op | source)
XLA Modules:
  0.0 176.3 jit_solution(6466143164559782731)
XLA Ops:
  6.5 1.0 dynamic-slice_bitcast_fusion.4
  7.6 3.3 %collective-permute-start.3 = (bf16[2,32,1024]{2,1,0:T(8,128)(2,1)S(1)}, bf16[2,32,1024]{2,1,0:T(8,128)(2,1)S(1)}, u32[]{:S(2)}, u32[]{:S(2)}) collective-permute-start(bf16[2,32,1024]{2,1,0:T(8,128)(2,1)S(1)} %pad_maximum_fusion.1), channel_id=1, source_target_pairs={{0,1},{1,0},{2,3},{3,2},{4,5},{5,4},{6,7},{7,6},{8,9},{9,8},{10,11... | collective-permute-start | bytes 393224 | tf_op jit(solution)/shard_map/ppermute | solution.py:218
  10.9 1.0 collective-permute-done.3
  12.6 0.9 slice.9
  13.6 1.1 collective-permute-start
  14.7 1.9 %copy-done.1 = bf16[3,256,2048]{2,1,0:T(8,128)(2,1)S(1)} copy-done((bf16[3,256,2048]{2,1,0:T(8,128)(2,1)S(1)}, bf16[3,256,2048]{2,1,0:T(8,128)(2,1)}, u32[]{:S(2)}) %copy-start.1) | copy-done | bytes 3145752
  16.6 0.9 copy-done.2
  17.4 2.7 %featurize.1 = (bf16[2048,256]{1,0:T(8,128)(2,1)S(1)}, bf16[2048,256]{1,0:T(8,128)(2,1)S(1)}, f32[3,8,2048]{2,1,0:T(8,128)S(1)}) custom-call(bf16[3,256,2048]{2,1,0:T(8,128)(2,1)S(1)} %copy-done.1, f32[3,3,2048]{2,1,0:T(4,128)S(1)} %copy-done.2), custom_call_target="tpu_custom_call" | custom-call | flops 20971520 | bytes 8388608 | tf_op jit(solution)/shard_map/featurize/pallas_call | solution.py:47
  20.2 3.4 %collective-permute-done.halo_ref = bf16[3,2,2048]{2,1,0:T(2,128)(2,1)S(1)} collective-permute-done((bf16[3,2,2048]{2,1,0:T(2,128)(2,1)S(1)}, bf16[3,2,2048]{2,1,0:T(2,128)(2,1)S(1)}, u32[]{:S(2)}, u32[]{:S(2)}) %collective-permute-start) | collective-permute-done | bytes 24608 | tf_op jit(solution)/shard_map/ppermute | solution.py:236
  23.6 1.6 join.1
  25.2 9.1 %all-to-all-start = ((bf16[64,32,256]{2,1,0:T(8,128)(2,1)}), bf16[64,32,256]{2,1,0:T(8,128)(2,1)S(1)}, u32[]{:S(2)}, u32[]{:S(2)}) async-start(bf16[64,32,256]{2,1,0:T(8,128)(2,1)} %bitcast.2), calls=%async_computation | async-start | bytes 2097152 | tf_op jit(solution)/shard_map/all_to_all | solution.py:241
  34.3 2.8 %collective-permute-start.1 = (bf16[32,32,256]{2,1,0:T(8,128)(2,1)S(1)}, bf16[32,32,256]{2,1,0:T(8,128)(2,1)S(1)}, u32[]{:S(2)}, u32[]{:S(2)}) collective-permute-start(bf16[32,32,256]{2,1,0:T(8,128)(2,1)S(1)} %dynamic-slice_bitcast_fusion), channel_id=1, source_target_pairs={{0,4},{4,0},{1,5},{5,1},{2,6},{6,2},{3,7},{7,3},{8,12},{12,8},{9,1... | collective-permute-start | bytes 1572872 | tf_op jit(solution)/shard_map/ppermute | solution.py:218
  37.3 17.7 %collective-permute-done.1.far_ref = bf16[32,32,256]{2,1,0:T(8,128)(2,1)S(1)} collective-permute-done((bf16[32,32,256]{2,1,0:T(8,128)(2,1)S(1)}, bf16[32,32,256]{2,1,0:T(8,128)(2,1)S(1)}, u32[]{:S(2)}, u32[]{:S(2)}) %collective-permute-start.1) | collective-permute-done | bytes 524320 | tf_op jit(solution)/shard_map/ppermute | solution.py:218
  54.9 15.0 %all-to-all-done.x_ref = bf16[64,32,256]{2,1,0:T(8,128)(2,1)S(1)} async-done(((bf16[64,32,256]{2,1,0:T(8,128)(2,1)}), bf16[64,32,256]{2,1,0:T(8,128)(2,1)S(1)}, u32[]{:S(2)}, u32[]{:S(2)}) %all-to-all-start) | async-done | bytes 1048608 | tf_op jit(solution)/shard_map/all_to_all | solution.py:241
  69.9 3.9 %toeplitz.1.t_ref = bf16[2,64,256,256]{3,2,1,0:T(8,128)(2,1)S(1)} custom-call(f32[2,1,16640]{2,1,0:T(1,128)S(1)} %broadcast_in_dim.11.h_ref), custom_call_target="tpu_custom_call" | custom-call | bytes 37748736 | tf_op jit(solution)/shard_map/toeplitz/pallas_call | solution.py:108
  73.8 9.9 %long_conv.1 = bf16[64,32,256]{2,1,0:T(8,128)(2,1)S(1)} custom-call(bf16[64,32,256]{2,1,0:T(8,128)(2,1)S(1)} %all-to-all-done.x_ref, bf16[2,64,256,256]{3,2,1,0:T(8,128)(2,1)S(1)} %toeplitz.1.t_ref), custom_call_target="tpu_custom_call" | custom-call | flops 8589934592 | bytes 20971520 | tf_op jit(solution)/shard_map/long_conv/pallas_call | solution.py:146
  83.7 44.4 %all_to_all.10.conv_ref = bf16[32,2,32,256]{3,2,1,0:T(8,128)(2,1)S(1)} all-to-all(bf16[32,2,32,256]{3,2,1,0:T(8,128)(2,1)S(1)} %bitcast.18), channel_id=1, replica_groups=mesh['z'=8,'y'=4,'xh'=2,'xl'=2,'core'=2] {'z','y'}, dimensions={0} | all-to-all | bytes 2097152 | tf_op jit(solution)/shard_map/all_to_all | solution.py:251
  128.5 3.1 %collective-permute-start.2 = (bf16[512,1024]{1,0:T(8,128)(2,1)S(1)}, bf16[512,1024]{1,0:T(8,128)(2,1)S(1)}, u32[]{:S(2)}, u32[]{:S(2)}) collective-permute-start(bf16[512,1024]{1,0:T(8,128)(2,1)S(1)} %gating.1.own_ref), channel_id=1, source_target_pairs={{0,1},{1,0},{2,3},{3,2},{4,5},{5,4},{6,7},{7,6},{8,9},{9,8},{10,11... | collective-permute-start | bytes 3145736 | tf_op jit(solution)/shard_map/ppermute | solution.py:218
  131.6 2.3 %collective-permute-done.2.other_ref = bf16[512,1024]{1,0:T(8,128)(2,1)S(1)} collective-permute-done((bf16[512,1024]{1,0:T(8,128)(2,1)S(1)}, bf16[512,1024]{1,0:T(8,128)(2,1)S(1)}, u32[]{:S(2)}, u32[]{:S(2)}) %collective-permute-start.2) | collective-permute-done | bytes 1048608 | tf_op jit(solution)/shard_map/ppermute | solution.py:218
  133.9 9.1 %all-gather.2.cloned.1.call-done.w_ref = bf16[32,2,2,32,1024]{4,3,2,1,0:T(8,128)(2,1)} async-done(((bf16[1,2,2,32,1024]{4,3,2,1,0:T(8,128)(2,1)}), bf16[32,2,2,32,1024]{4,3,2,1,0:T(8,128)(2,1)}) %all-gather.2.cloned.1.call-update) | async-done | bytes 8388624 | tf_op jit(solution)/shard_map/all_gather | solution.py:232
  143.0 3.4 %copy-done = bf16[32,2,2,32,1024]{4,3,2,1,0:T(8,128)(2,1)S(1)} copy-done((bf16[32,2,2,32,1024]{4,3,2,1,0:T(8,128)(2,1)S(1)}, bf16[32,2,2,32,1024]{4,3,2,1,0:T(8,128)(2,1)}, u32[]{:S(2)}) %copy-start) | copy-done | bytes 8388632
  146.4 1.2 project.5
  147.7 1.2 collective-permute-start.7
  148.9 1.3 collective-permute-start.5
  150.2 2.3 %project.4 = (bf16[128,1024]{1,0:T(8,128)(2,1)S(1)}, bf16[128,1024]{1,0:T(8,128)(2,1)S(1)}, bf16[128,1024]{1,0:T(8,128)(2,1)S(1)}, bf16[128,1024]{1,0:T(8,128)(2,1)S(1)}) custom-call(bf16[512,1024]{1,0:T(8,128)(2,1)S(1)} %gating.1.own_ref, bf16[512,1024]{1,0:T(8,128)(2,1)S(1)} %collective-permute-done.2.other_ref, bf16[32,2,2,32,1024]{4,3,2,1,0:T(8,128)(2,1)S(1)} %copy-done), custom_call_target="tpu_custom_call" | custom-call | flops 2147483648 | bytes 6291456 | tf_op jit(solution)/shard_map/project/pallas_call | solution.py:204
  153.2 0.9 collective-permute-start.9
  154.5 2.9 %collective-permute-start.8 = (bf16[128,1024]{1,0:T(8,128)(2,1)S(1)}, bf16[128,1024]{1,0:T(8,128)(2,1)S(1)}, u32[]{:S(2)}, u32[]{:S(2)}) collective-permute-start(bf16[128,1024]{1,0:T(8,128)(2,1)S(1)} %add_convert_fusion.1), channel_id=1, source_target_pairs={{0,6},{6,0},{2,4},{4,2},{1,7},{7,1},{3,5},{5,3},{8,14},{14,8},{10,... | collective-permute-start | bytes 786440 | tf_op jit(solution)/shard_map/ppermute | solution.py:267
  157.5 1.2 project.3
  158.8 2.0 %collective-permute-done.4 = bf16[128,1024]{1,0:T(8,128)(2,1)S(1)} collective-permute-done((bf16[128,1024]{1,0:T(8,128)(2,1)S(1)}, bf16[128,1024]{1,0:T(8,128)(2,1)S(1)}, u32[]{:S(2)}, u32[]{:S(2)}) %collective-permute-start.4) | collective-permute-done | bytes 262176 | tf_op jit(solution)/shard_map/ppermute | solution.py:262
  160.8 2.0 %collective-permute-done.9 = bf16[128,1024]{1,0:T(8,128)(2,1)S(1)} collective-permute-done((bf16[128,1024]{1,0:T(8,128)(2,1)S(1)}, bf16[128,1024]{1,0:T(8,128)(2,1)S(1)}, u32[]{:S(2)}, u32[]{:S(2)}) %collective-permute-start.9) | collective-permute-done | bytes 262176 | tf_op jit(solution)/shard_map/ppermute | solution.py:263
  162.8 5.6 %collective-permute-done.8 = bf16[128,1024]{1,0:T(8,128)(2,1)S(1)} collective-permute-done((bf16[128,1024]{1,0:T(8,128)(2,1)S(1)}, bf16[128,1024]{1,0:T(8,128)(2,1)S(1)}, u32[]{:S(2)}, u32[]{:S(2)}) %collective-permute-start.8) | collective-permute-done | bytes 262176 | tf_op jit(solution)/shard_map/ppermute | solution.py:267
  168.4 1.1 add_convert_fusion
  (21 shorter events, 2.6 us)
Async XLA Ops:
  6.5 30.6 %copy-start.3 = (f32[2,16384]{1,0:T(2,128)S(1)}, f32[2,16384]{1,0:T(2,128)}, u32[]{:S(2)}) copy-start(f32[2,16384]{1,0:T(2,128)} %param.6) | copy-start | bytes 393220
  6.5 136.5 %all-gather.2.cloned.1.call-start = ((), (), s32[]{:S(2)}) async-start(), calls=%async_computation.2 | async-start | bytes 8650752 | tf_op jit(solution)/shard_map/all_gather | solution.py:232
  7.6 4.3 %collective-permute-start.3 = (bf16[2,32,1024]{2,1,0:T(8,128)(2,1)S(1)}, bf16[2,32,1024]{2,1,0:T(8,128)(2,1)S(1)}, u32[]{:S(2)}, u32[]{:S(2)}) collective-permute-start(bf16[2,32,1024]{2,1,0:T(8,128)(2,1)S(1)} %pad_maximum_fusion.1), channel_id=1, source_target_pairs={{0,1},{1,0},{2,3},{3,2},{4,5},{5,4},{6,7},{7,6},{8,9},{9,8},{10,11... | collective-permute-start | bytes 393224 | tf_op jit(solution)/shard_map/ppermute | solution.py:218
  13.6 10.0 %collective-permute-start = (bf16[3,2,2048]{2,1,0:T(2,128)(2,1)S(1)}, bf16[3,2,2048]{2,1,0:T(2,128)(2,1)S(1)}, u32[]{:S(2)}, u32[]{:S(2)}) collective-permute-start(bf16[3,2,2048]{2,1,0:T(2,128)(2,1)S(1)} %slice.9), channel_id=1, source_target_pairs={{0,4},{4,8},{8,12},{12,16},{16,20},{20,24},{24,28},{28,32},{32,36}... | collective-permute-start | bytes 73736 | tf_op jit(solution)/shard_map/ppermute | solution.py:236
  14.7 1.9 %copy-start.1 = (bf16[3,256,2048]{2,1,0:T(8,128)(2,1)S(1)}, bf16[3,256,2048]{2,1,0:T(8,128)(2,1)}, u32[]{:S(2)}) copy-start(bf16[3,256,2048]{2,1,0:T(8,128)(2,1)} %x_ref.1) | copy-start | bytes 9437188
  16.5 0.9 copy-start.2
  25.2 44.7 %all-to-all-start = ((bf16[64,32,256]{2,1,0:T(8,128)(2,1)}), bf16[64,32,256]{2,1,0:T(8,128)(2,1)S(1)}, u32[]{:S(2)}, u32[]{:S(2)}) async-start(bf16[64,32,256]{2,1,0:T(8,128)(2,1)} %bitcast.2), calls=%async_computation | async-start | bytes 2097152 | tf_op jit(solution)/shard_map/all_to_all | solution.py:241
  34.3 20.6 %collective-permute-start.1 = (bf16[32,32,256]{2,1,0:T(8,128)(2,1)S(1)}, bf16[32,32,256]{2,1,0:T(8,128)(2,1)S(1)}, u32[]{:S(2)}, u32[]{:S(2)}) collective-permute-start(bf16[32,32,256]{2,1,0:T(8,128)(2,1)S(1)} %dynamic-slice_bitcast_fusion), channel_id=1, source_target_pairs={{0,4},{4,0},{1,5},{5,1},{2,6},{6,2},{3,7},{7,3},{8,12},{12,8},{9,1... | collective-permute-start | bytes 1572872 | tf_op jit(solution)/shard_map/ppermute | solution.py:218
  128.5 5.4 %collective-permute-start.2 = (bf16[512,1024]{1,0:T(8,128)(2,1)S(1)}, bf16[512,1024]{1,0:T(8,128)(2,1)S(1)}, u32[]{:S(2)}, u32[]{:S(2)}) collective-permute-start(bf16[512,1024]{1,0:T(8,128)(2,1)S(1)} %gating.1.own_ref), channel_id=1, source_target_pairs={{0,1},{1,0},{2,3},{3,2},{4,5},{5,4},{6,7},{7,6},{8,9},{9,8},{10,11... | collective-permute-start | bytes 3145736 | tf_op jit(solution)/shard_map/ppermute | solution.py:218
  143.0 3.4 %copy-start = (bf16[32,2,2,32,1024]{4,3,2,1,0:T(8,128)(2,1)S(1)}, bf16[32,2,2,32,1024]{4,3,2,1,0:T(8,128)(2,1)}, u32[]{:S(2)}) copy-start(bf16[32,2,2,32,1024]{4,3,2,1,0:T(8,128)(2,1)} %all-gather.2.cloned.1.call-done.w_ref) | copy-start | bytes 25165828
  147.7 6.7 %collective-permute-start.7 = (bf16[128,1024]{1,0:T(8,128)(2,1)S(1)}, bf16[128,1024]{1,0:T(8,128)(2,1)S(1)}, u32[]{:S(2)}, u32[]{:S(2)}) collective-permute-start(bf16[128,1024]{1,0:T(8,128)(2,1)S(1)} %get-tuple-element.31), channel_id=1, source_target_pairs={{0,2},{2,0},{4,6},{6,4},{1,3},{3,1},{5,7},{7,5},{8,10},{10,8},{12,... | collective-permute-start | bytes 786440 | tf_op jit(solution)/shard_map/ppermute | solution.py:259
  148.9 8.5 %collective-permute-start.5 = (bf16[128,1024]{1,0:T(8,128)(2,1)S(1)}, bf16[128,1024]{1,0:T(8,128)(2,1)S(1)}, u32[]{:S(2)}, u32[]{:S(2)}) collective-permute-start(bf16[128,1024]{1,0:T(8,128)(2,1)S(1)} %get-tuple-element.29), channel_id=1, source_target_pairs={{0,6},{6,0},{2,4},{4,2},{1,7},{7,1},{3,5},{5,3},{8,14},{14,8},{10,... | collective-permute-start | bytes 786440 | tf_op jit(solution)/shard_map/ppermute | solution.py:260
  152.5 8.3 %collective-permute-start.4 = (bf16[128,1024]{1,0:T(8,128)(2,1)S(1)}, bf16[128,1024]{1,0:T(8,128)(2,1)S(1)}, u32[]{:S(2)}, u32[]{:S(2)}) collective-permute-start(bf16[128,1024]{1,0:T(8,128)(2,1)S(1)} %get-tuple-element.27), channel_id=1, source_target_pairs={{0,2},{2,0},{4,6},{6,4},{1,3},{3,1},{5,7},{7,5},{8,10},{10,8},{12,... | collective-permute-start | bytes 786440 | tf_op jit(solution)/shard_map/ppermute | solution.py:262
  153.2 9.6 %collective-permute-start.9 = (bf16[128,1024]{1,0:T(8,128)(2,1)S(1)}, bf16[128,1024]{1,0:T(8,128)(2,1)S(1)}, u32[]{:S(2)}, u32[]{:S(2)}) collective-permute-start(bf16[128,1024]{1,0:T(8,128)(2,1)S(1)} %get-tuple-element.32), channel_id=1, source_target_pairs={{0,6},{6,0},{2,4},{4,2},{1,7},{7,1},{3,5},{5,3},{8,14},{14,8},{10,... | collective-permute-start | bytes 786440 | tf_op jit(solution)/shard_map/ppermute | solution.py:263
  154.5 13.9 %collective-permute-start.8 = (bf16[128,1024]{1,0:T(8,128)(2,1)S(1)}, bf16[128,1024]{1,0:T(8,128)(2,1)S(1)}, u32[]{:S(2)}, u32[]{:S(2)}) collective-permute-start(bf16[128,1024]{1,0:T(8,128)(2,1)S(1)} %add_convert_fusion.1), channel_id=1, source_target_pairs={{0,6},{6,0},{2,4},{4,2},{1,7},{7,1},{3,5},{5,3},{8,14},{14,8},{10,... | collective-permute-start | bytes 786440 | tf_op jit(solution)/shard_map/ppermute | solution.py:267
  157.4 11.0 %collective-permute-start.6 = (bf16[128,1024]{1,0:T(8,128)(2,1)S(1)}, bf16[128,1024]{1,0:T(8,128)(2,1)S(1)}, u32[]{:S(2)}, u32[]{:S(2)}) collective-permute-start(bf16[128,1024]{1,0:T(8,128)(2,1)S(1)} %add_convert_fusion.2), channel_id=1, source_target_pairs={{0,2},{2,0},{4,6},{6,4},{1,3},{3,1},{5,7},{7,5},{8,10},{10,8},{12,... | collective-permute-start | bytes 786440 | tf_op jit(solution)/shard_map/ppermute | solution.py:266
Sparse Core Ops, SparseCore 0:
  12.8 130.2 all-gather.1

commit v4 on v3

--- a/solution.py
+++ b/solution.py
@@ -166,11 +166,13 @@
     half = half_ref[0]
     for r in range(2):
         for c in range(srcs // group):
-            some = slice(c * group, (c + 1) * group)
-            conv = conv_ref[some, half if r == 0 else 1 - half].astype(F32)
-            gate = near_ref[some, half] if r == 0 else far_ref[some]
-            gated = (conv * gate.astype(F32)).astype(BF16).astype(F32)
-            gated = gated.reshape(group * chans, tok).T.astype(BF16)
+            parts = []
+            for d in range(group):
+                src = d * (srcs // group) + c
+                conv = conv_ref[src, half if r == 0 else 1 - half].astype(F32)
+                gate = near_ref[src, half] if r == 0 else far_ref[src]
+                parts.append((conv * gate.astype(F32)).astype(BF16).astype(F32))
+            gated = jnp.concatenate(parts, 0).T.astype(BF16)
             out_ref[r * tok : (r + 1) * tok, c * group * chans : (c + 1) * group * chans] = gated
 
 
@@ -224,12 +226,12 @@
     xh, xl, core = lax.axis_index("xh"), lax.axis_index("xl"), lax.axis_index("core")
     pick = functools.partial(lax.dynamic_index_in_dim, keepdims=False)
 
-    def columns(lane, core):
-        return lax.dynamic_slice_in_dim(out_weight, (lane * 2 + core) * (wide // 4), wide // 4, 1)
-
-    given = swap(jnp.stack([columns(xl, 1 - core), columns(1 - xl, 1 - core)]), "core")
-    rows = jnp.stack([columns(xl, core), given[0], columns(1 - xl, core), given[1]])
-    weights = lax.all_gather(rows.reshape(2, 2, deep, wide // 4), ("z", "y"), axis=0)
+    def columns(weight, lane):
+        return lax.dynamic_slice_in_dim(weight, (lane * 2 + core) * (wide // 4), wide // 4, 1)
+
+    given = swap(out_weight, "core")
+    rows = jnp.stack([columns(w, lane) for lane in (xl, 1 - xl) for w in (out_weight, given)])
+    weights = lax.all_gather(rows.reshape(2, 2, deep, wide // 4), ("y", "z"), axis=0)
 
     rim = features[:, tok - 2 :, :]
     ctx_size = lax.axis_size(CTX)

time: 177 us -> 176 us (level)
  no operation moved by 1% of the time
where the time goes in v4:
time: 176 us
  waiting for transfers between devices  57.6 us (33%)
  blocking collectives  45.1 us (26%)
  starting transfers between devices  26.3 us (15%)
  Pallas kernels  23.3 us (13%)
  between operations  13.5 us (8%)
  local copies, waits for them, and re-layouts  8.16 us (5%)
  other arithmetic  1.93 us (1%)
    all_to_all x1, blocking collectives, on_device(): lax.all_to_all(convolved, ('z', 'y'), split_axis=0, concat_axis=0, tiled=...  45.1 us
    ppermute x3, waiting for transfers between devices, swap(): return lax.ppermute(x, axis, [(0, 1), (1, 0)])  20.5 us
    all_to_all x1, waiting for transfers between devices, on_device(): lax.all_to_all(product.reshape(ctx_size, mine, tok), CTX, split_axis=0, c...  14.7 us
    pallas_call x1, Pallas kernels, long_conv(): pl.pallas_call(conv_kernel, in_specs=[VM, VM], out_specs=VM, out_shape=ja...  9.88 us
    all_gather x1, waiting for transfers between devices, on_device(): lax.all_gather(rows.reshape(2, 2, deep, wide // 4), ('y', 'z'), axis=0)  9.25 us
    all_to_all x1, starting transfers between devices, on_device(): lax.all_to_all(product.reshape(ctx_size, mine, tok), CTX, split_axis=0, c...  9.06 us
    ppermute x3, starting transfers between devices, swap(): return lax.ppermute(x, axis, [(0, 1), (1, 0)])  9 us
    unnamed x8, local copies, waits for them, and re-layouts  6.17 us
  transfers between devices with their start and end apart: 12, of which 10 were waited for; matrix products, arithmetic and copies ran while one was open for 1% of the time, Pallas kernels for 13%

profile of v4, /device:TPU:1, one launch (start us, length us, event | category | flops | bytes accessed | tf_op | source)
XLA Modules:
  0.0 175.9 jit_solution(4878733935422646378)
XLA Ops:
  6.5 3.2 %collective-permute-start.3 = (bf16[32,4096]{1,0:T(8,128)(2,1)}, bf16[32,4096]{1,0:T(8,128)(2,1)S(1)}, u32[]{:S(2)}, u32[]{:S(2)}) collective-permute-start(bf16[32,4096]{1,0:T(8,128)(2,1)} %param.7), channel_id=1, source_target_pairs={{0,1},{1,0},{2,3},{3,2},{4,5},{5,4},{6,7},{7,6},{8,9},{9,8},{10,11... | collective-permute-start | bytes 786440 | tf_op jit(solution)/shard_map/ppermute | solution.py:220
  9.8 0.9 dynamic-slice_bitcast_fusion.4
  11.2 0.7 pad_maximum_fusion
  11.9 0.9 slice.3
  12.9 1.1 collective-permute-start
  13.9 1.9 %copy-done.1 = bf16[3,256,2048]{2,1,0:T(8,128)(2,1)S(1)} copy-done((bf16[3,256,2048]{2,1,0:T(8,128)(2,1)S(1)}, bf16[3,256,2048]{2,1,0:T(8,128)(2,1)}, u32[]{:S(2)}) %copy-start.1) | copy-done | bytes 3145752
  15.8 0.9 copy-done.2
  16.7 2.7 %featurize.1 = (bf16[2048,256]{1,0:T(8,128)(2,1)S(1)}, bf16[2048,256]{1,0:T(8,128)(2,1)S(1)}, f32[3,8,2048]{2,1,0:T(8,128)S(1)}) custom-call(bf16[3,256,2048]{2,1,0:T(8,128)(2,1)S(1)} %copy-done.1, f32[3,3,2048]{2,1,0:T(4,128)S(1)} %copy-done.2), custom_call_target="tpu_custom_call" | custom-call | flops 20971520 | bytes 8388608 | tf_op jit(solution)/shard_map/featurize/pallas_call | solution.py:47
  19.5 3.4 %collective-permute-done.halo_ref = bf16[3,2,2048]{2,1,0:T(2,128)(2,1)S(1)} collective-permute-done((bf16[3,2,2048]{2,1,0:T(2,128)(2,1)S(1)}, bf16[3,2,2048]{2,1,0:T(2,128)(2,1)S(1)}, u32[]{:S(2)}, u32[]{:S(2)}) %collective-permute-start) | collective-permute-done | bytes 24608 | tf_op jit(solution)/shard_map/ppermute | solution.py:238
  22.9 1.6 join.1
  24.5 9.1 %all-to-all-start = ((bf16[64,32,256]{2,1,0:T(8,128)(2,1)}), bf16[64,32,256]{2,1,0:T(8,128)(2,1)S(1)}, u32[]{:S(2)}, u32[]{:S(2)}) async-start(bf16[64,32,256]{2,1,0:T(8,128)(2,1)} %bitcast.2), calls=%async_computation | async-start | bytes 2097152 | tf_op jit(solution)/shard_map/all_to_all | solution.py:243
  33.6 2.8 %collective-permute-start.1 = (bf16[32,32,256]{2,1,0:T(8,128)(2,1)S(1)}, bf16[32,32,256]{2,1,0:T(8,128)(2,1)S(1)}, u32[]{:S(2)}, u32[]{:S(2)}) collective-permute-start(bf16[32,32,256]{2,1,0:T(8,128)(2,1)S(1)} %dynamic-slice_bitcast_fusion), channel_id=1, source_target_pairs={{0,4},{4,0},{1,5},{5,1},{2,6},{6,2},{3,7},{7,3},{8,12},{12,8},{9,1... | collective-permute-start | bytes 1572872 | tf_op jit(solution)/shard_map/ppermute | solution.py:220
  36.6 17.7 %collective-permute-done.1.far_ref = bf16[32,32,256]{2,1,0:T(8,128)(2,1)S(1)} collective-permute-done((bf16[32,32,256]{2,1,0:T(8,128)(2,1)S(1)}, bf16[32,32,256]{2,1,0:T(8,128)(2,1)S(1)}, u32[]{:S(2)}, u32[]{:S(2)}) %collective-permute-start.1) | collective-permute-done | bytes 524320 | tf_op jit(solution)/shard_map/ppermute | solution.py:220
  54.2 14.7 %all-to-all-done.x_ref = bf16[64,32,256]{2,1,0:T(8,128)(2,1)S(1)} async-done(((bf16[64,32,256]{2,1,0:T(8,128)(2,1)}), bf16[64,32,256]{2,1,0:T(8,128)(2,1)S(1)}, u32[]{:S(2)}, u32[]{:S(2)}) %all-to-all-start) | async-done | bytes 1048608 | tf_op jit(solution)/shard_map/all_to_all | solution.py:243
  68.9 3.9 %toeplitz.1.t_ref = bf16[2,64,256,256]{3,2,1,0:T(8,128)(2,1)S(1)} custom-call(f32[2,1,16640]{2,1,0:T(1,128)S(1)} %broadcast_in_dim.11.h_ref), custom_call_target="tpu_custom_call" | custom-call | bytes 37748736 | tf_op jit(solution)/shard_map/toeplitz/pallas_call | solution.py:108
  72.8 9.9 %long_conv.1 = bf16[64,32,256]{2,1,0:T(8,128)(2,1)S(1)} custom-call(bf16[64,32,256]{2,1,0:T(8,128)(2,1)S(1)} %all-to-all-done.x_ref, bf16[2,64,256,256]{3,2,1,0:T(8,128)(2,1)S(1)} %toeplitz.1.t_ref), custom_call_target="tpu_custom_call" | custom-call | flops 8589934592 | bytes 20971520 | tf_op jit(solution)/shard_map/long_conv/pallas_call | solution.py:146
  82.7 45.1 %all_to_all.10.conv_ref = bf16[32,2,32,256]{3,2,1,0:T(8,128)(2,1)S(1)} all-to-all(bf16[32,2,32,256]{3,2,1,0:T(8,128)(2,1)S(1)} %bitcast.18), channel_id=1, replica_groups=mesh['z'=8,'y'=4,'xh'=2,'xl'=2,'core'=2] {'z','y'}, dimensions={0} | all-to-all | bytes 2097152 | tf_op jit(solution)/shard_map/all_to_all | solution.py:253
  128.2 3.0 %collective-permute-start.2 = (bf16[512,1024]{1,0:T(8,128)(2,1)S(1)}, bf16[512,1024]{1,0:T(8,128)(2,1)S(1)}, u32[]{:S(2)}, u32[]{:S(2)}) collective-permute-start(bf16[512,1024]{1,0:T(8,128)(2,1)S(1)} %gating.1.own_ref), channel_id=1, source_target_pairs={{0,1},{1,0},{2,3},{3,2},{4,5},{5,4},{6,7},{7,6},{8,9},{9,8},{10,11... | collective-permute-start | bytes 3145736 | tf_op jit(solution)/shard_map/ppermute | solution.py:220
  131.2 2.3 %collective-permute-done.2.other_ref = bf16[512,1024]{1,0:T(8,128)(2,1)S(1)} collective-permute-done((bf16[512,1024]{1,0:T(8,128)(2,1)S(1)}, bf16[512,1024]{1,0:T(8,128)(2,1)S(1)}, u32[]{:S(2)}, u32[]{:S(2)}) %collective-permute-start.2) | collective-permute-done | bytes 1048608 | tf_op jit(solution)/shard_map/ppermute | solution.py:220
  133.5 9.3 %all-gather.2.cloned.1.call-done.w_ref = bf16[32,2,2,32,1024]{4,3,2,1,0:T(8,128)(2,1)} async-done(((bf16[1,2,2,32,1024]{4,3,2,1,0:T(8,128)(2,1)}), bf16[32,2,2,32,1024]{4,3,2,1,0:T(8,128)(2,1)}) %all-gather.2.cloned.1.call-update) | async-done | bytes 8388624 | tf_op jit(solution)/shard_map/all_gather | solution.py:234
  142.7 3.4 %copy-done = bf16[32,2,2,32,1024]{4,3,2,1,0:T(8,128)(2,1)S(1)} copy-done((bf16[32,2,2,32,1024]{4,3,2,1,0:T(8,128)(2,1)S(1)}, bf16[32,2,2,32,1024]{4,3,2,1,0:T(8,128)(2,1)}, u32[]{:S(2)}) %copy-start) | copy-done | bytes 8388632
  146.1 1.2 project.5
  147.4 1.4 collective-permute-start.7
  148.8 1.1 collective-permute-start.5
  149.9 2.3 %project.4 = (bf16[128,1024]{1,0:T(8,128)(2,1)S(1)}, bf16[128,1024]{1,0:T(8,128)(2,1)S(1)}, bf16[128,1024]{1,0:T(8,128)(2,1)S(1)}, bf16[128,1024]{1,0:T(8,128)(2,1)S(1)}) custom-call(bf16[512,1024]{1,0:T(8,128)(2,1)S(1)} %gating.1.own_ref, bf16[512,1024]{1,0:T(8,128)(2,1)S(1)} %collective-permute-done.2.other_ref, bf16[32,2,2,32,1024]{4,3,2,1,0:T(8,128)(2,1)S(1)} %copy-done), custom_call_target="tpu_custom_call" | custom-call | flops 2147483648 | bytes 6291456 | tf_op jit(solution)/shard_map/project/pallas_call | solution.py:206
  152.8 1.2 collective-permute-start.9
  154.2 2.8 %collective-permute-start.8 = (bf16[128,1024]{1,0:T(8,128)(2,1)S(1)}, bf16[128,1024]{1,0:T(8,128)(2,1)S(1)}, u32[]{:S(2)}, u32[]{:S(2)}) collective-permute-start(bf16[128,1024]{1,0:T(8,128)(2,1)S(1)} %add_convert_fusion.1), channel_id=1, source_target_pairs={{0,6},{6,0},{2,4},{4,2},{1,7},{7,1},{3,5},{5,3},{8,14},{14,8},{10,... | collective-permute-start | bytes 786440 | tf_op jit(solution)/shard_map/ppermute | solution.py:269
  157.2 1.2 project.3
  158.5 2.1 %collective-permute-done.4 = bf16[128,1024]{1,0:T(8,128)(2,1)S(1)} collective-permute-done((bf16[128,1024]{1,0:T(8,128)(2,1)S(1)}, bf16[128,1024]{1,0:T(8,128)(2,1)S(1)}, u32[]{:S(2)}, u32[]{:S(2)}) %collective-permute-start.4) | collective-permute-done | bytes 262176 | tf_op jit(solution)/shard_map/ppermute | solution.py:264
  160.5 1.9 %collective-permute-done.9 = bf16[128,1024]{1,0:T(8,128)(2,1)S(1)} collective-permute-done((bf16[128,1024]{1,0:T(8,128)(2,1)S(1)}, bf16[128,1024]{1,0:T(8,128)(2,1)S(1)}, u32[]{:S(2)}, u32[]{:S(2)}) %collective-permute-start.9) | collective-permute-done | bytes 262176 | tf_op jit(solution)/shard_map/ppermute | solution.py:265
  162.4 5.6 %collective-permute-done.8 = bf16[128,1024]{1,0:T(8,128)(2,1)S(1)} collective-permute-done((bf16[128,1024]{1,0:T(8,128)(2,1)S(1)}, bf16[128,1024]{1,0:T(8,128)(2,1)S(1)}, u32[]{:S(2)}, u32[]{:S(2)}) %collective-permute-start.8) | collective-permute-done | bytes 262176 | tf_op jit(solution)/shard_map/ppermute | solution.py:269
  168.0 1.1 add_convert_fusion
  (20 shorter events, 2.1 us)
Async XLA Ops:
  6.5 29.9 %copy-start.3 = (f32[2,16384]{1,0:T(2,128)S(1)}, f32[2,16384]{1,0:T(2,128)}, u32[]{:S(2)}) copy-start(f32[2,16384]{1,0:T(2,128)} %param.6) | copy-start | bytes 393220
  6.5 136.2 %all-gather.2.cloned.1.call-start = ((), (), s32[]{:S(2)}) async-start(), calls=%async_computation.2 | async-start | bytes 8650752 | tf_op jit(solution)/shard_map/all_gather | solution.py:234
  6.5 4.6 %collective-permute-start.3 = (bf16[32,4096]{1,0:T(8,128)(2,1)}, bf16[32,4096]{1,0:T(8,128)(2,1)S(1)}, u32[]{:S(2)}, u32[]{:S(2)}) collective-permute-start(bf16[32,4096]{1,0:T(8,128)(2,1)} %param.7), channel_id=1, source_target_pairs={{0,1},{1,0},{2,3},{3,2},{4,5},{5,4},{6,7},{7,6},{8,9},{9,8},{10,11... | collective-permute-start | bytes 786440 | tf_op jit(solution)/shard_map/ppermute | solution.py:220
  12.9 10.0 %collective-permute-start = (bf16[3,2,2048]{2,1,0:T(2,128)(2,1)S(1)}, bf16[3,2,2048]{2,1,0:T(2,128)(2,1)S(1)}, u32[]{:S(2)}, u32[]{:S(2)}) collective-permute-start(bf16[3,2,2048]{2,1,0:T(2,128)(2,1)S(1)} %slice.3), channel_id=1, source_target_pairs={{0,4},{4,8},{8,12},{12,16},{16,20},{20,24},{24,28},{28,32},{32,36}... | collective-permute-start | bytes 73736 | tf_op jit(solution)/shard_map/ppermute | solution.py:238
  13.9 1.9 %copy-start.1 = (bf16[3,256,2048]{2,1,0:T(8,128)(2,1)S(1)}, bf16[3,256,2048]{2,1,0:T(8,128)(2,1)}, u32[]{:S(2)}) copy-start(bf16[3,256,2048]{2,1,0:T(8,128)(2,1)} %x_ref.1) | copy-start | bytes 9437188
  15.8 0.9 copy-start.2
  24.5 44.4 %all-to-all-start = ((bf16[64,32,256]{2,1,0:T(8,128)(2,1)}), bf16[64,32,256]{2,1,0:T(8,128)(2,1)S(1)}, u32[]{:S(2)}, u32[]{:S(2)}) async-start(bf16[64,32,256]{2,1,0:T(8,128)(2,1)} %bitcast.2), calls=%async_computation | async-start | bytes 2097152 | tf_op jit(solution)/shard_map/all_to_all | solution.py:243
  33.6 20.6 %collective-permute-start.1 = (bf16[32,32,256]{2,1,0:T(8,128)(2,1)S(1)}, bf16[32,32,256]{2,1,0:T(8,128)(2,1)S(1)}, u32[]{:S(2)}, u32[]{:S(2)}) collective-permute-start(bf16[32,32,256]{2,1,0:T(8,128)(2,1)S(1)} %dynamic-slice_bitcast_fusion), channel_id=1, source_target_pairs={{0,4},{4,0},{1,5},{5,1},{2,6},{6,2},{3,7},{7,3},{8,12},{12,8},{9,1... | collective-permute-start | bytes 1572872 | tf_op jit(solution)/shard_map/ppermute | solution.py:220
  128.2 5.3 %collective-permute-start.2 = (bf16[512,1024]{1,0:T(8,128)(2,1)S(1)}, bf16[512,1024]{1,0:T(8,128)(2,1)S(1)}, u32[]{:S(2)}, u32[]{:S(2)}) collective-permute-start(bf16[512,1024]{1,0:T(8,128)(2,1)S(1)} %gating.1.own_ref), channel_id=1, source_target_pairs={{0,1},{1,0},{2,3},{3,2},{4,5},{5,4},{6,7},{7,6},{8,9},{9,8},{10,11... | collective-permute-start | bytes 3145736 | tf_op jit(solution)/shard_map/ppermute | solution.py:220
  142.7 3.4 %copy-start = (bf16[32,2,2,32,1024]{4,3,2,1,0:T(8,128)(2,1)S(1)}, bf16[32,2,2,32,1024]{4,3,2,1,0:T(8,128)(2,1)}, u32[]{:S(2)}) copy-start(bf16[32,2,2,32,1024]{4,3,2,1,0:T(8,128)(2,1)} %all-gather.2.cloned.1.call-done.w_ref) | copy-start | bytes 25165828
  147.4 6.7 %collective-permute-start.7 = (bf16[128,1024]{1,0:T(8,128)(2,1)S(1)}, bf16[128,1024]{1,0:T(8,128)(2,1)S(1)}, u32[]{:S(2)}, u32[]{:S(2)}) collective-permute-start(bf16[128,1024]{1,0:T(8,128)(2,1)S(1)} %get-tuple-element.31), channel_id=1, source_target_pairs={{0,2},{2,0},{4,6},{6,4},{1,3},{3,1},{5,7},{7,5},{8,10},{10,8},{12,... | collective-permute-start | bytes 786440 | tf_op jit(solution)/shard_map/ppermute | solution.py:261
  148.8 8.3 %collective-permute-start.5 = (bf16[128,1024]{1,0:T(8,128)(2,1)S(1)}, bf16[128,1024]{1,0:T(8,128)(2,1)S(1)}, u32[]{:S(2)}, u32[]{:S(2)}) collective-permute-start(bf16[128,1024]{1,0:T(8,128)(2,1)S(1)} %get-tuple-element.29), channel_id=1, source_target_pairs={{0,6},{6,0},{2,4},{4,2},{1,7},{7,1},{3,5},{5,3},{8,14},{14,8},{10,... | collective-permute-start | bytes 786440 | tf_op jit(solution)/shard_map/ppermute | solution.py:262
  152.2 8.3 %collective-permute-start.4 = (bf16[128,1024]{1,0:T(8,128)(2,1)S(1)}, bf16[128,1024]{1,0:T(8,128)(2,1)S(1)}, u32[]{:S(2)}, u32[]{:S(2)}) collective-permute-start(bf16[128,1024]{1,0:T(8,128)(2,1)S(1)} %get-tuple-element.27), channel_id=1, source_target_pairs={{0,2},{2,0},{4,6},{6,4},{1,3},{3,1},{5,7},{7,5},{8,10},{10,8},{12,... | collective-permute-start | bytes 786440 | tf_op jit(solution)/shard_map/ppermute | solution.py:264
  152.8 9.6 %collective-permute-start.9 = (bf16[128,1024]{1,0:T(8,128)(2,1)S(1)}, bf16[128,1024]{1,0:T(8,128)(2,1)S(1)}, u32[]{:S(2)}, u32[]{:S(2)}) collective-permute-start(bf16[128,1024]{1,0:T(8,128)(2,1)S(1)} %get-tuple-element.32), channel_id=1, source_target_pairs={{0,6},{6,0},{2,4},{4,2},{1,7},{7,1},{3,5},{5,3},{8,14},{14,8},{10,... | collective-permute-start | bytes 786440 | tf_op jit(solution)/shard_map/ppermute | solution.py:265
  154.2 13.8 %collective-permute-start.8 = (bf16[128,1024]{1,0:T(8,128)(2,1)S(1)}, bf16[128,1024]{1,0:T(8,128)(2,1)S(1)}, u32[]{:S(2)}, u32[]{:S(2)}) collective-permute-start(bf16[128,1024]{1,0:T(8,128)(2,1)S(1)} %add_convert_fusion.1), channel_id=1, source_target_pairs={{0,6},{6,0},{2,4},{4,2},{1,7},{7,1},{3,5},{5,3},{8,14},{14,8},{10,... | collective-permute-start | bytes 786440 | tf_op jit(solution)/shard_map/ppermute | solution.py:269
  157.1 10.9 %collective-permute-start.6 = (bf16[128,1024]{1,0:T(8,128)(2,1)S(1)}, bf16[128,1024]{1,0:T(8,128)(2,1)S(1)}, u32[]{:S(2)}, u32[]{:S(2)}) collective-permute-start(bf16[128,1024]{1,0:T(8,128)(2,1)S(1)} %add_convert_fusion.2), channel_id=1, source_target_pairs={{0,2},{2,0},{4,6},{6,4},{1,3},{3,1},{5,7},{7,5},{8,10},{10,8},{12,... | collective-permute-start | bytes 786440 | tf_op jit(solution)/shard_map/ppermute | solution.py:268
Sparse Core Ops, SparseCore 0:
  12.1 130.6 all-gather.1
